TPU v7x, 32 devices: a whole 2x2x4 slice. The times are simulated.
32 devices in a mesh: gx: 2 (over core), gy: 4 (over y, x), gz: 4 (over z).
Axes of the slice: x: 2, y: 2, z: 4, core: 2. Of those that a mesh axis runs over, the one named last changes fastest.
Arguments:
- field: float32 [128, 128, 2048], P('gz', 'gx', 'gy'), may hold values from -6 to 6
Outputs:
- coeffs: float32 [128, 128, 2048], P('gz', 'gx', 'gy')
All inputs are finite; a program needn't handle non-finite values.
Results may differ from a plain program's by a relative error of at most 0.000075.
Values sent between devices are 32-bit elements; how exact they have to be, the bound alone decides.
No kernel may reach another device: no remote copies, remote signals or barrier semaphores. Data moves between devices by JAX's collectives and lax.ppermute only.
A program may use at most 128 MiB of HBM per device.

v0:
```python
import functools

import jax
import jax.numpy as jnp
import ml_dtypes
import numpy as np
from jax import lax
from jax.experimental import pallas as pl
from jax.experimental.pallas import tpu as pltpu
from jax.sharding import PartitionSpec as P

lift_alpha = -1.586134342
lift_beta = -0.05298011854
lift_gamma = 0.8829110762
lift_delta = 0.4435068522
lift_zeta = 1.149604398

BF = jnp.bfloat16
F32 = jnp.float32
MIB = 1024 * 1024


def periodic_lift(u):
    s, d = u[0::2].copy(), u[1::2].copy()
    d = d + lift_alpha * (s + np.roll(s, -1, 0))
    s = s + lift_beta * (np.roll(d, 1, 0) + d)
    d = d + lift_gamma * (s + np.roll(s, -1, 0))
    s = s + lift_delta * (np.roll(d, 1, 0) + d)
    out = np.empty_like(u)
    out[0::2] = s * lift_zeta
    out[1::2] = d / lift_zeta
    return out


@functools.lru_cache(None)
def blocks(n):
    current = np.eye(4 * n)
    found = []
    for level in range(3):
        full = periodic_lift(current)
        m = n >> level
        rows = full[m : 2 * m]
        found.append((rows[:, n : 2 * n], rows[:, :n], rows[:, 2 * n : 3 * n]))
        current = full[0::2]
    return found


def row_space(outer, rank):
    _, sizes, basis = np.linalg.svd(outer, full_matrices=False)
    assert sizes[rank:].max() < 1e-10
    basis = basis[:rank].copy()
    basis[np.abs(basis) < 1e-12] = 0.0
    return basis


LEFT_RANKS = (2, 3, 4)
RIGHT_RANKS = (2, 3, 3)


@functools.lru_cache(None)
def sides(n):
    out = []
    for level, (main, left, right) in enumerate(blocks(n)):
        cl = row_space(left, LEFT_RANKS[level])
        cr = row_space(right, RIGHT_RANKS[level])
        out.append((main, cl, left @ cl.T, cr, right @ cr.T))
    return out


@functools.lru_cache(None)
def joint_sides(n):
    found = blocks(n)
    cl = row_space(np.concatenate([b[1] for b in found]), 6)
    cr = row_space(np.concatenate([b[2] for b in found]), 6)
    maps = [(b[0], b[1] @ cl.T, b[2] @ cr.T) for b in found]
    return cl, cr, maps


def hi_lo(table):
    table = np.asarray(table, np.float32)
    hi = table.astype(ml_dtypes.bfloat16)
    lo = (table - hi.astype(np.float32)).astype(ml_dtypes.bfloat16)
    return hi, lo


def stack_lhs(table):
    hi, lo = hi_lo(table)
    return np.concatenate([hi, lo, hi], axis=1)


def stack_rhs(table):
    hi, lo = hi_lo(table)
    return np.concatenate([hi, hi, lo], axis=0)


def split(values):
    hi = values.astype(BF)
    return hi, (values - hi.astype(F32)).astype(BF)


def dot(a, b):
    return lax.dot_general(a, b, (((1,), (0,)), ((), ())), preferred_element_type=F32)


def dot_t(a, b):
    return lax.dot_general(a, b, (((1,), (1,)), ((), ())), preferred_element_type=F32)


def spread_columns(table, step, width):
    out = np.zeros((table.shape[0], width))
    out[:, ::step] = table
    return out


VM = pl.BlockSpec(memory_space=pltpu.VMEM)


def vmem(shape, dtype=F32):
    return pltpu.VMEM(shape, dtype)


def params(mib):
    return pltpu.CompilerParams(vmem_limit_bytes=mib * MIB)


def x_send(field):
    nz, nx, ny = field.shape
    cl, cr, _ = joint_sides(nx)
    one = stack_lhs(np.concatenate([cl, cr]))
    pair = np.zeros((24, 6 * nx), one.dtype)
    pair[:12, : 3 * nx] = one
    pair[12:, 3 * nx :] = one
    step = 8

    def kernel(u_ref, c_ref, out_ref):
        table = c_ref[...]
        for p in range(step // 2):
            parts = []
            for z in (2 * p, 2 * p + 1):
                hi, lo = split(u_ref[z])
                parts += [hi, hi, lo]
            out_ref[24 * p : 24 * p + 24, :] = dot(table, jnp.concatenate(parts, axis=0))

    return pl.pallas_call(
        kernel,
        grid=(nz // step,),
        in_specs=[pl.BlockSpec((step, nx, ny), lambda i: (i, 0, 0)), VM],
        out_specs=pl.BlockSpec((12 * step, ny), lambda i: (i, 0)),
        out_shape=jax.ShapeDtypeStruct((nz * 12, ny), F32),
        compiler_params=params(16),
        name="x_send",
    )(field, jnp.asarray(pair))


def x_exchange(message):
    count = lax.axis_size("gx")
    right = [(i, (i + 1) % count) for i in range(count)]
    if count == 2:
        return lax.ppermute(message, "gx", right)
    left = [(j, i) for i, j in right]
    rows, ny = message.shape
    grid = message.reshape(rows // 12, 12, ny)
    from_left = lax.ppermute(grid[:, :6], "gx", right)
    from_right = lax.ppermute(grid[:, 6:], "gx", left)
    return jnp.concatenate([from_left, from_right], axis=1).reshape(rows, ny)


def x_apply(field, halo):
    nz, nx, ny = field.shape
    _, _, maps = joint_sides(nx)
    main = np.concatenate([m for m, _, _ in maps])
    outer = np.concatenate([np.concatenate([l, r], axis=1) for _, l, r in maps])
    pad = np.zeros((main.shape[0], 4))
    tables = np.stack(
        [
            stack_lhs(np.concatenate([main, outer, pad], axis=1)),
            stack_lhs(np.concatenate([main, pad, outer], axis=1)),
        ]
    )
    rows = main.shape[0]
    counts = [nx, nx // 2, nx // 4]
    step = 8
    steps = nz // step

    combos = []
    for level, (_, cl, _, cr, _) in enumerate(sides(ny)):
        both = np.zeros((8, 128))
        assert np.abs(cl[:, : ny - 64]).max() == 0 and np.abs(cr[:, 64:]).max() == 0
        both[: cl.shape[0], 64:] = cl[:, ny - 64 :]
        both[4 : 4 + cr.shape[0], :64] = cr[:, :64]
        combos.append(stack_lhs(both))
    combos = np.stack(combos)

    def kernel(u_ref, r_ref, t_ref, c_ref, x1, x2, x3, right_ref, left_ref, e1, e2, e3):
        i = pl.program_id(0)
        lanes = lax.broadcasted_iota(jnp.int32, (rows, 128), 1)
        for z in range(step):
            start = pl.multiple_of(i * (12 * step) + 24 * (z // 2) + 8 * (z % 2), 8)
            hi, lo = split(u_ref[z])
            rhi, rlo = split(r_ref[pl.ds(start, 16), :])
            stacked = jnp.concatenate([hi, rhi, hi, rhi, lo, rlo], axis=0)
            got = dot(t_ref[z % 2], stacked)
            edge = jnp.where(lanes < 64, got[:, :128], got[:, ny - 128 :])
            ehi, elo = split(edge)
            estack = jnp.concatenate([ehi, ehi, elo], axis=1)
            at = 0
            for ref, eref, n in zip((x1, x2, x3), (e1, e2, e3), counts):
                where = pl.ds(pl.multiple_of((i * step + z) * n, 16), n)
                ref[where, :] = got[at : at + n]
                eref[where, :] = estack[at : at + n]
                at += n

        @pl.when(i == steps - 1)
        def _():
            row = 0
            for level, (eref, n) in enumerate(zip((e1, e2, e3), counts)):
                got = dot_t(c_ref[level], eref[...])
                for j in range(nz * n // 512):
                    for c in range(LEFT_RANKS[level]):
                        right_ref[row : row + 1, :] = got[c : c + 1, 512 * j : 512 * j + 512]
                        if c < RIGHT_RANKS[level]:
                            left_ref[row : row + 1, :] = got[4 + c : 5 + c, 512 * j : 512 * j + 512]
                        else:
                            left_ref[row : row + 1, :] = jnp.zeros((1, 512), F32)
                        row += 1
            right_ref[row:, :] = jnp.zeros((24 - row, 512), F32)
            left_ref[row:, :] = jnp.zeros((24 - row, 512), F32)

    return pl.pallas_call(
        kernel,
        grid=(steps,),
        in_specs=[pl.BlockSpec((step, nx, ny), lambda i: (i, 0, 0)), VM, VM, VM],
        out_specs=[VM] * 5,
        out_shape=[vmem((nz * n, ny)) for n in counts] + [jax.ShapeDtypeStruct((24, 512), F32)] * 2,
        scratch_shapes=[pltpu.VMEM((nz * n, 384), BF) for n in counts],
        compiler_params=params(24),
        name="x_apply",
    )(field, halo, jnp.asarray(tables), jnp.asarray(combos))


def z_tables(nz):
    out = []
    for _, cl, pl_, cr, pr in sides(nz):
        out.append((np.concatenate([cl, cr]), np.concatenate([pl_, pr], axis=1)))
    return out


def weighted(parts):
    total = None
    for scalar, get in parts:
        if abs(scalar) < 1e-12:
            continue
        term = get() * np.float32(scalar)
        total = term if total is None else total + term
    return total


def z_combine(xs, nz):
    ny = xs[0].shape[1]
    tables = [t for t, _ in z_tables(nz)]
    counts = [x.shape[0] // nz for x in xs]

    def kernel(x1, x2, x3, o1, o2, o3):
        for ref, out, table, n in zip((x1, x2, x3), (o1, o2, o3), tables, counts):

            def body(k, _, ref=ref, out=out, table=table, n=n):
                row = pl.multiple_of((k // (ny // 128)) * 8, 8)
                lane = pl.multiple_of((k % (ny // 128)) * 128, 128)
                get = {}
                for z in range(nz):
                    if np.abs(table[:, z]).max() > 1e-12:
                        get[z] = ref[pl.ds(pl.multiple_of(z * n + row, 8), 8), pl.ds(lane, 128)]
                for c in range(table.shape[0]):
                    out[pl.ds(pl.multiple_of(c * n + row, 8), 8), pl.ds(lane, 128)] = weighted(
                        [(table[c, z], lambda z=z: get[z]) for z in range(nz)]
                    )
                return 0

            lax.fori_loop(0, (n // 8) * (ny // 128), body, 0)

    return pl.pallas_call(
        kernel,
        in_specs=[VM] * 3,
        out_specs=[VM] * 3,
        out_shape=[vmem((t.shape[0] * n, ny)) for t, n in zip(tables, counts)],
        compiler_params=params(16),
        cost_estimate=pl.CostEstimate(flops=20_000_000, bytes_accessed=6_000_000, transcendentals=0),
        name="z_combine",
    )(*xs)


def y_tables(ny, spread):
    out = []
    for level, (main, _, left, _, right) in enumerate(sides(ny)):
        step = (1 << level) if spread else 1
        width = ny if spread else ny >> level
        fit = lambda t: spread_columns(t.T, step, width)
        out.append((fit(main), fit(left), fit(right)))
    return out


def halo_rows(level, chunk, nz, counts):
    start = 0
    for below in range(level):
        start += (nz * counts[below] // 512) * LEFT_RANKS[below]
    return start + chunk * LEFT_RANKS[level]


def halo_table(left, right, level, chunks, nz, counts):
    base = np.zeros((48, left.shape[1]))
    for chunk in chunks:
        row = halo_rows(level, chunk, nz, counts)
        base[row : row + left.shape[0]] = left
        base[24 + row : 24 + row + right.shape[0]] = right
    hi, lo = hi_lo(base)
    none = np.zeros((32, left.shape[1]), hi.dtype)
    return np.concatenate([hi, hi, none, lo, np.zeros_like(hi), none])


def turned(left_ref, right_ref):
    both = jnp.concatenate([left_ref[...], right_ref[...]], axis=0)
    hi = both.astype(BF).astype(F32)
    wide = jnp.concatenate([hi, both - hi, jnp.zeros((32, 512), F32)], axis=0)
    return wide.T


def y_messages(combined, from_left, from_right, nz):
    ny = combined[0].shape[1]
    tables = z_tables(nz)
    nums = [t.shape[0] for t, _ in tables]
    counts = [c.shape[0] // n for c, n in zip(combined, nums)]
    mains, halos, coefs = [], [], []
    for level, (main, left, right) in enumerate(y_tables(ny, False)):
        mains.append(stack_rhs(main))
        chunks = nz * counts[level] // 512
        halos.append(halo_table(left, right, level, range(chunks), nz, counts))
        per = 512 // counts[level]
        table = tables[level][0]
        coef = np.zeros((nums[level], per, 128), np.float32)
        for c in range(nums[level]):
            for zz in range(per):
                for chunk in range(chunks):
                    row = halo_rows(level, chunk, nz, counts)
                    for lane in range(LEFT_RANKS[level]):
                        for base in (0, 24, 48, 72):
                            coef[c, zz, base + row + lane] = table[c, chunk * per + zz]
        coefs.append(coef.reshape(nums[level] * per, 128))
    heights = [(nums[0] // 2) * counts[0], 3 * counts[1] // 2, 4 * counts[2] // 4]
    height = sum(heights)
    height += -height % 8

    def kernel(c1, c2, c3, fl, fr, m1, m2, m3, h1, h2, h3, k1, k2, k3, right_ref, left_ref):
        halo = turned(fl, fr)
        got = []
        for c_ref, m, h, k, n, num in zip(
            (c1, c2, c3), (m1, m2, m3), (h1, h2, h3), (k1, k2, k3), counts, nums
        ):
            per = 512 // n
            extra = []
            for c in range(num):
                total = None
                for zz in range(per):
                    term = halo[zz * n : zz * n + n] * k[c * per + zz : c * per + zz + 1, :]
                    total = term if total is None else total + term
                extra.append(total)
            ehi, elo = split(jnp.concatenate(extra, axis=0))
            hi, lo = split(c_ref[...])
            got.append(
                dot(jnp.concatenate([hi, lo, hi], axis=1), m[...])
                + dot(jnp.concatenate([ehi, ehi], axis=1), h[...])
                + dot(elo, h[:128])
            )
        for side, ref in enumerate((right_ref, left_ref)):
            at = 0
            for level in range(3):
                n, width = counts[level], ny >> level
                ranks = LEFT_RANKS if side == 0 else RIGHT_RANKS
                first = 0 if side == 0 else LEFT_RANKS[level] * n
                total = ranks[level] * n
                per_row = ny // width
                tall = heights[level]
                for part in range(per_row):
                    use = min(tall, total - part * tall)
                    if use > 0:
                        ref[at : at + use, part * width : (part + 1) * width] = got[level][
                            first + part * tall : first + part * tall + use
                        ]
                    if use < tall:
                        use = max(use, 0)
                        ref[at + use : at + tall, part * width : (part + 1) * width] = jnp.zeros(
                            (tall - use, width), F32
                        )
                at += tall
            if at < height:
                ref[at:, :] = jnp.zeros((height - at, ny), F32)

    return pl.pallas_call(
        kernel,
        in_specs=[VM] * 14,
        out_specs=[VM] * 2,
        out_shape=[jax.ShapeDtypeStruct((height, ny), F32)] * 2,
        compiler_params=params(24),
        name="y_messages",
    )(
        *combined,
        from_left,
        from_right,
        *[jnp.asarray(t) for t in mains],
        *[jnp.asarray(t) for t in halos],
        *[jnp.asarray(t) for t in coefs],
    )


def add(a, b):
    if a is None:
        return b
    return a if b is None else a + b


def scale(a, c):
    return None if a is None else a * np.float32(c)


def open_lift(values, first, last):
    get = values.get
    low, high = first // 2 - 3, last // 2 + 4
    s = {i: get(2 * i) for i in range(low, high + 1)}
    d = {i: get(2 * i + 1) for i in range(low, high + 1)}
    pick = lambda t, i: t.get(i)
    d1 = {i: add(d[i], scale(add(s[i], pick(s, i + 1)), lift_alpha)) for i in range(low, high + 1)}
    s1 = {i: add(s[i], scale(add(pick(d1, i - 1), d1[i]), lift_beta)) for i in range(low, high + 1)}
    d2 = {i: add(d1[i], scale(add(s1[i], pick(s1, i + 1)), lift_gamma)) for i in range(low, high + 1)}
    s2 = {i: add(s1[i], scale(add(pick(d2, i - 1), d2[i]), lift_delta)) for i in range(low, high + 1)}
    out = {}
    for z in range(first, last + 1):
        if z % 2:
            out[z] = scale(d2[z // 2], 1.0 / lift_zeta)
        else:
            out[z] = scale(s2[z // 2], lift_zeta)
    return out


def main_part(xs, from_left, from_right, nz):
    ny = xs[0].shape[1]
    counts = [x.shape[0] // nz for x in xs]
    mains, halos = [], []
    for level, (main, left, right) in enumerate(y_tables(ny, True)):
        mains.append(stack_rhs(main))
        chunks = nz * counts[level] // 512
        halos.append(
            np.stack([halo_table(left, right, level, [c], nz, counts) for c in range(chunks)])
        )

    def kernel(x1, x2, x3, fl, fr, m1, m2, m3, h1, h2, h3, out_ref, y1, y2, y3, w2, halo_ref):
        halo = turned(fl, fr).astype(BF)
        halo_ref[...] = jnp.concatenate([halo, halo], axis=1)
        for x, m, h, y, n in zip((x1, x2, x3), (m1, m2, m3), (h1, h2, h3), (y1, y2, y3), counts):

            def chunk_body(j, _, x=x, m=m, h=h, y=y):
                where = pl.ds(pl.multiple_of(j * 512, 512), 512)
                hi, lo = split(x[where, :])
                y[where, :] = dot(jnp.concatenate([hi, lo, hi], axis=1), m[...]) + dot(
                    halo_ref[...], h[j]
                )
                return 0

            lax.fori_loop(0, nz * n // 512, chunk_body, 0)

        groups = ny // 128

        def place(k):
            return pl.multiple_of((k // groups) * 8, 8), pl.multiple_of((k % groups) * 128, 128)

        def loaded(ref, n, row, lane):
            return {
                z: ref[pl.ds(pl.multiple_of(z * n + row, 8), 8), pl.ds(lane, 128)] for z in range(nz)
            }

        def level_one(k, _):
            row, lane = place(k)
            got = open_lift(loaded(y1, counts[0], row, lane), 0, nz - 1)
            for z in range(nz):
                out_ref[k % groups, z, pl.ds(row, 8), :] = got[z]
            return 0

        lax.fori_loop(0, (counts[0] // 8) * groups, level_one, 0)

        def lows(values, first, last):
            got = open_lift(values, 2 * first, 2 * last)
            return {i: got[2 * i] for i in range(first, last + 1) if got[2 * i] is not None}

        def level_two(k, _):
            row, lane = place(k)
            one = lows(loaded(y2, counts[1], row, lane), -2, nz // 2 + 1)
            got = open_lift(one, 0, nz // 2 - 1)
            for z in range(nz // 2):
                w2[k % groups, pl.ds(pl.multiple_of(z * counts[1] + row, 8), 8), :] = got[z]
            return 0

        lax.fori_loop(0, (counts[1] // 8) * groups, level_two, 0)

        lane_ids = lax.broadcasted_iota(jnp.int32, (8, 128), 1)

        def level_three(k, _):
            row, lane = place(k)
            one = lows(loaded(y3, counts[2], row, lane), -2, nz // 2 + 1)
            two = lows(one, -3, nz // 4 + 2)
            got = open_lift(two, 0, nz // 4 - 1)
            for z in range(nz // 4):
                where = pl.ds(2 * z * counts[1] + 2 * row, 8, stride=2)
                old = w2[k % groups, where, :]
                w2[k % groups, where, :] = jnp.where(lane_ids % 4 == 0, got[z], old)
            return 0

        lax.fori_loop(0, (counts[2] // 8) * groups, level_three, 0)

        def merge(k, _):
            row, _ = place(k)
            for z in range(nz // 2):
                inner = w2[k % groups, pl.ds(pl.multiple_of(z * counts[1] + row, 8), 8), :]
                where = pl.ds(2 * row, 8, stride=2)
                old = out_ref[k % groups, 2 * z, where, :]
                out_ref[k % groups, 2 * z, where, :] = jnp.where(lane_ids % 2 == 0, inner, old)
            return 0

        lax.fori_loop(0, (counts[1] // 8) * groups, merge, 0)

    return pl.pallas_call(
        kernel,
        in_specs=[VM] * 11,
        out_specs=VM,
        out_shape=vmem((ny // 128, nz, counts[0], 128)),
        scratch_shapes=[pltpu.VMEM((nz * n, ny), F32) for n in counts]
        + [pltpu.VMEM((ny // 128, nz // 2 * counts[1], 128), F32), pltpu.VMEM((512, 256), BF)],
        compiler_params=params(32),
        cost_estimate=pl.CostEstimate(
            flops=8_000_000_000, bytes_accessed=20_000_000, transcendentals=0
        ),
        name="main_part",
    )(*xs, from_left, from_right, *[jnp.asarray(t) for t in mains], *[jnp.asarray(t) for t in halos])


def z_apply(inner, from_left, from_right):
    groups, nz, nx, _ = inner.shape
    ny = groups * 128
    maps = [p for _, p in z_tables(nz)]
    counts = [nx, nx // 2, nx // 4]
    tables = []
    for level in (1, 2):
        width = ny >> level
        hi = spread_columns(np.eye(width), 1 << level, ny).astype(ml_dtypes.bfloat16)
        tables.append(np.concatenate([hi, hi]))
    heights = [2 * counts[0], 3 * counts[1] // 2, 4 * counts[2] // 4]
    step = 4

    def kernel(in_ref, fl, fr, t2, t3, out_ref, s1, s2, s3):
        i = pl.program_id(0)

        @pl.when(i == 0)
        def _():
            row_ids = lax.broadcasted_iota(jnp.int32, (nx, ny), 0)
            lane_ids = lax.broadcasted_iota(jnp.int32, (nx, ny), 1)
            inside = ((row_ids % 2) + (lane_ids % 2)) == 0
            s2[...] = jnp.zeros(s2.shape, F32)
            s3[...] = jnp.zeros(s3.shape, F32)
            for side, ref in enumerate((fl, fr)):
                ranks = LEFT_RANKS if side == 0 else RIGHT_RANKS
                for c in range(2):
                    outside = jnp.where(inside, 0.0, ref[c * nx : c * nx + nx, :])
                    for q in range(groups):
                        s1[2 * side + c, q] = outside[:, 128 * q : 128 * q + 128]
                at = heights[0]
                for level, table, to in ((1, t2, s2), (2, t3, s3)):
                    width, tall, n = ny >> level, heights[level], counts[level]
                    flat = jnp.concatenate(
                        [ref[at : at + tall, p * width : p * width + width] for p in range(1 << level)],
                        axis=0,
                    )
                    hi, lo = split(flat)
                    got = dot(jnp.concatenate([hi, lo], axis=1), table[...])
                    first = 0 if side == 0 else LEFT_RANKS[level]
                    for c in range(ranks[level]):
                        for q in range(groups):
                            to[first + c, q, pl.ds(0, n, stride=1 << level), :] = got[
                                c * n : c * n + n, 128 * q : 128 * q + 128
                            ]
                    at += tall

        for z_out in range(nz):

            @pl.when(i == z_out // step)
            def _(z=z_out):
                def body(k, _):
                    q = k % groups
                    row = pl.multiple_of((k // groups) * 8, 8)
                    lane = pl.multiple_of(q * 128, 128)
                    value = in_ref[q, z % step, pl.ds(row, 8), :]
                    extra = None
                    for c in range(4):
                        scalar = maps[0][z, c]
                        if abs(scalar) < 1e-12:
                            continue
                        if z % 2:
                            start = pl.multiple_of((c % 2) * nx + row, 8)
                            term = (fl, fr)[c // 2][pl.ds(start, 8), pl.ds(lane, 128)]
                        else:
                            term = s1[c, q, pl.ds(row, 8), :]
                        extra = add(extra, term * np.float32(scalar))
                    if z % 2 == 0:
                        for c in range(maps[1].shape[1]):
                            scalar = maps[1][z // 2, c]
                            if abs(scalar) > 1e-12:
                                extra = add(extra, s2[c, q, pl.ds(row, 8), :] * np.float32(scalar))
                    if z % 4 == 0:
                        ids = (
                            lax.broadcasted_iota(jnp.int32, (8, 128), 0) % 4
                            + lax.broadcasted_iota(jnp.int32, (8, 128), 1) % 4
                        )
                        third = None
                        for c in range(maps[2].shape[1]):
                            if abs(maps[2][z // 4, c]) > 1e-12:
                                third = add(third, s3[c, q, pl.ds(row, 8), :] * np.float32(maps[2][z // 4, c]))
                        if third is None:
                            third = jnp.zeros((8, 128), F32)
                        if extra is None:
                            extra = jnp.zeros((8, 128), F32)
                        extra = jnp.where(ids == 0, third, extra)
                    if extra is not None:
                        value = value + extra
                    out_ref[z % step, pl.ds(row, 8), pl.ds(lane, 128)] = value
                    return 0

                lax.fori_loop(0, (nx // 8) * groups, body, 0)

    return pl.pallas_call(
        kernel,
        grid=(nz // step,),
        in_specs=[pl.BlockSpec((groups, step, nx, 128), lambda i: (0, i, 0, 0)), VM, VM, VM, VM],
        out_specs=pl.BlockSpec((step, nx, ny), lambda i: (i, 0, 0)),
        out_shape=jax.ShapeDtypeStruct((nz, nx, ny), F32),
        scratch_shapes=[pltpu.VMEM((m.shape[1], groups, nx, 128), F32) for m in maps],
        compiler_params=params(24),
        name="z_apply",
    )(inner, from_left, from_right, *[jnp.asarray(t) for t in tables])


def swap(to_right, to_left, axis):
    count = lax.axis_size(axis)
    right = [(i, (i + 1) % count) for i in range(count)]
    left = [(j, i) for i, j in right]
    return lax.ppermute(to_right, axis, right), lax.ppermute(to_left, axis, left)


def local(field):
    nz = field.shape[0]
    halo = x_exchange(x_send(field))
    x1, x2, x3, to_right, to_left = x_apply(field, halo)
    from_left, from_right = swap(to_right, to_left, "gy")
    combined = z_combine((x1, x2, x3), nz)
    to_right, to_left = y_messages(combined, from_left, from_right, nz)
    below, above = swap(to_right, to_left, "gz")
    inner = main_part((x1, x2, x3), from_left, from_right, nz)
    return z_apply(inner, below, above)


def solution(mesh):
    placed = (P("gz", "gx", "gy"),)
    return jax.shard_map(
        local, mesh=mesh, in_specs=placed, out_specs=P("gz", "gx", "gy"), check_vma=False
    )
```

profile of v0, /device:TPU:0, one launch (start us, length us, event | category | flops | bytes accessed | tf_op | source)
XLA Modules:
  0.0 54.4 jit_solution(14134284613602137943)
XLA Ops:
  0.0 0.0 copy-start.13
  0.0 0.0 copy-start
  0.0 2.2 %copy-done = f32[32,64,512]{2,1,0:T(8,128)S(1)} copy-done((f32[32,64,512]{2,1,0:T(8,128)S(1)}, f32[32,64,512]{2,1,0:T(8,128)}, u32[]{:S(2)}) %copy-start) | copy-done | bytes 4194328
  2.2 0.7 %copy-done.14 = bf16[24,384]{1,0:T(8,128)(2,1)S(1)} copy-done((bf16[24,384]{1,0:T(8,128)(2,1)S(1)}, bf16[24,384]{1,0:T(8,128)(2,1)}, u32[]{:S(2)}) %copy-start.14) | copy-done | bytes 18456
  2.9 1.5 %x_send.1 = f32[384,512]{1,0:T(8,128)S(1)} custom-call(f32[32,64,512]{2,1,0:T(8,128)S(1)} %copy-done, bf16[24,384]{1,0:T(8,128)(2,1)S(1)} %copy-done.14), custom_call_target="tpu_custom_call" | custom-call | tf_op jit(solution)/shard_map/x_send/pallas_call | solution.py:144
  4.5 0.5 collective-permute-start
  5.0 1.9 %collective-permute-done.r_ref = f32[384,512]{1,0:T(8,128)S(1)} collective-permute-done((f32[384,512]{1,0:T(8,128)S(1)}, f32[384,512]{1,0:T(8,128)S(1)}, u32[]{:S(2)}, u32[]{:S(2)}) %collective-permute-start) | collective-permute-done | bytes 786464 | tf_op jit(solution)/shard_map/ppermute | solution.py:159
  6.9 0.0 copy-done.13
  6.9 0.0 copy-done.1
  6.9 0.0 copy-done.10
  6.9 2.6 %x_apply.1 = (f32[2048,512]{1,0:T(8,128)S(1)}, f32[1024,512]{1,0:T(8,128)S(1)}, f32[512,512]{1,0:T(8,128)S(1)}, f32[24,512]{1,0:T(8,128)S(1)}, f32[24,512]{1,0:T(8,128)S(1)}) custom-call(f32[32,64,512]{2,1,0:T(8,128)S(1)} %copy-done.1, f32[384,512]{1,0:T(8,128)S(1)} %collective-permute-done.r_ref, bf16[2,112,240]{2,1,0:T(8,128)(2,1)S(1)} %copy-done.10, ...), custom_call_target="tpu_custom_call" | custom-call | tf_op jit(solution)/shard_map/x_apply/pallas_call | solution.py:229
  9.5 0.0 copy-start.3
  9.5 0.0 copy-start.5
  9.5 0.0 copy-start.7
  9.5 0.0 copy-start.8
  9.6 0.0 copy-start.9
  9.6 0.0 copy-start.11
  9.6 0.0 copy-start.12
  9.6 0.0 copy-start.15
  9.6 2.9 %collective-permute-start.1 = (f32[24,512]{1,0:T(8,128)S(1)}, f32[24,512]{1,0:T(8,128)S(1)}, u32[]{:S(2)}, u32[]{:S(2)}) collective-permute-start(f32[24,512]{1,0:T(8,128)S(1)} %get-tuple-element.18), channel_id=1, source_target_pairs={{0,4},{4,8},{8,12},{12,0},{1,5},{5,9},{9,13},{13,1},{2,6},{6,10},{... | collective-permute-start | bytes 147464 | tf_op jit(solution)/shard_map/ppermute | solution.py:651
  12.5 1.0 %collective-permute-start.2 = (f32[24,512]{1,0:T(8,128)S(1)}, f32[24,512]{1,0:T(8,128)S(1)}, u32[]{:S(2)}, u32[]{:S(2)}) collective-permute-start(f32[24,512]{1,0:T(8,128)S(1)} %get-tuple-element.19), channel_id=1, source_target_pairs={{4,0},{8,4},{12,8},{0,12},{5,1},{9,5},{13,9},{1,13},{6,2},{10,6},{... | collective-permute-start | bytes 147464 | tf_op jit(solution)/shard_map/ppermute | solution.py:651
  13.6 0.0 copy-start.20
  13.6 2.2 %z_combine.1 = (f32[256,512]{1,0:T(8,128)S(1)}, f32[192,512]{1,0:T(8,128)S(1)}, f32[112,512]{1,0:T(8,128)S(1)}) custom-call(f32[2048,512]{1,0:T(8,128)S(1)} %get-tuple-element.15.x1, f32[1024,512]{1,0:T(8,128)S(1)} %get-tuple-element.16.x2, f32[512,512]{1,0:T(8,128)S(1)} %get-tuple-element.17.x3), custom_call_target="tpu_custom_call" | custom-call | flops 20000000 | bytes 6000000 | tf_op jit(solution)/shard_map/z_combine/pallas_call | solution.py:281
  15.7 0.0 collective-permute-done.1.fl
  15.8 1.1 %collective-permute-done.2.fr = f32[24,512]{1,0:T(8,128)S(1)} collective-permute-done((f32[24,512]{1,0:T(8,128)S(1)}, f32[24,512]{1,0:T(8,128)S(1)}, u32[]{:S(2)}, u32[]{:S(2)}) %collective-permute-start.2) | collective-permute-done | bytes 49184 | tf_op jit(solution)/shard_map/ppermute | solution.py:651
  16.8 0.0 copy-done.2
  16.8 0.0 copy-done.3
  16.8 0.0 copy-done.5
  16.8 0.0 copy-done.7
  16.8 0.0 copy-done.8
  16.8 0.0 copy-done.9
  16.9 0.0 copy-done.11
  16.9 0.0 copy-done.12
  16.9 0.0 copy-done.15
  16.9 1.1 %y_messages.1 = (f32[192,512]{1,0:T(8,128)S(1)}, f32[192,512]{1,0:T(8,128)S(1)}) custom-call(f32[256,512]{1,0:T(8,128)S(1)} %get-tuple-element.20.c1, f32[192,512]{1,0:T(8,128)S(1)} %get-tuple-element.21.c2, f32[112,512]{1,0:T(8,128)S(1)} %get-tuple-element.22.c3, f32[24,512]{1,0:T(8,128)S(1)} %collective-permute-done.1.fl, ...), custom_call_target="tpu_custom_call" | custom-call | tf_op jit(solution)/shard_map/y_messages/pallas_call | solution.py:397
  18.0 1.6 %collective-permute-start.3 = (f32[192,512]{1,0:T(8,128)S(1)}, f32[192,512]{1,0:T(8,128)S(1)}, u32[]{:S(2)}, u32[]{:S(2)}) collective-permute-start(f32[192,512]{1,0:T(8,128)S(1)} %get-tuple-element.23), channel_id=1, source_target_pairs={{0,1},{1,2},{2,3},{3,0},{4,5},{5,6},{6,7},{7,4},{8,9},{9,10},{10,1... | collective-permute-start | bytes 1179656 | tf_op jit(solution)/shard_map/ppermute | solution.py:651
  19.7 2.2 %collective-permute-start.4 = (f32[192,512]{1,0:T(8,128)S(1)}, f32[192,512]{1,0:T(8,128)S(1)}, u32[]{:S(2)}, u32[]{:S(2)}) collective-permute-start(f32[192,512]{1,0:T(8,128)S(1)} %get-tuple-element.24), channel_id=1, source_target_pairs={{1,0},{2,1},{3,2},{0,3},{5,4},{6,5},{7,6},{4,7},{9,8},{10,9},{11,1... | collective-permute-start | bytes 1179656 | tf_op jit(solution)/shard_map/ppermute | solution.py:651
  21.9 0.0 copy-done.16
  21.9 0.0 copy-done.17
  21.9 0.0 copy-done.18
  21.9 0.0 copy-done.19
  21.9 0.0 copy-done.20
  21.9 12.9 %main_part.1.in_ref = f32[4,32,64,128]{3,2,1,0:T(8,128)S(1)} custom-call(f32[2048,512]{1,0:T(8,128)S(1)} %get-tuple-element.15.x1, f32[1024,512]{1,0:T(8,128)S(1)} %get-tuple-element.16.x2, f32[512,512]{1,0:T(8,128)S(1)} %get-tuple-element.17.x3, f32[24,512]{1,0:T(8,128)S(1)} %collective-permute-done.1.fl, f32[24,512]{1,0:T(8,128)S(1)} %collective-permute-done.2.fr, ...), custom_call_target="tpu_custom_call" | custom-call | flops 8000000000 | bytes 20000000 | tf_op jit(solution)/shard_map/main_part/pallas_call | solution.py:528
  34.8 0.0 collective-permute-done.3.fl
  34.8 3.3 %collective-permute-done.4.fr = f32[192,512]{1,0:T(8,128)S(1)} collective-permute-done((f32[192,512]{1,0:T(8,128)S(1)}, f32[192,512]{1,0:T(8,128)S(1)}, u32[]{:S(2)}, u32[]{:S(2)}) %collective-permute-start.4) | collective-permute-done | bytes 393248 | tf_op jit(solution)/shard_map/ppermute | solution.py:651
  38.1 0.0 copy-done.4
  38.1 0.0 copy-done.6
  38.1 16.3 %z_apply.1 = f32[32,64,512]{2,1,0:T(8,128)} custom-call(f32[4,32,64,128]{3,2,1,0:T(8,128)S(1)} %main_part.1.in_ref, f32[192,512]{1,0:T(8,128)S(1)} %collective-permute-done.3.fl, f32[192,512]{1,0:T(8,128)S(1)} %collective-permute-done.4.fr, bf16[512,512]{1,0:T(8,128)(2,1)S(1)} %copy-done.4, bf16[256,512]{1,0:T(8,128)(2,1)S(1)} %copy-done.6), custom_call_target="tpu_custom_call" | custom-call | tf_op jit(solution)/shard_map/z_apply/pallas_call | solution.py:635
  (10 shorter events, 0.0 us)
Async XLA Ops:
  0.0 6.9 %copy-start.13 = (bf16[3,8,384]{2,1,0:T(8,128)(2,1)S(1)}, bf16[3,8,384]{2,1,0:T(8,128)(2,1)}, u32[]{:S(2)}) copy-start(bf16[3,8,384]{2,1,0:T(8,128)(2,1)} %constant.40.clone.c_ref) | copy-start | bytes 55300
  0.0 2.2 %copy-start = (f32[32,64,512]{2,1,0:T(8,128)S(1)}, f32[32,64,512]{2,1,0:T(8,128)}, u32[]{:S(2)}) copy-start(f32[32,64,512]{2,1,0:T(8,128)} %u_ref.3) | copy-start | bytes 12582916
  2.2 0.7 %copy-start.14 = (bf16[24,384]{1,0:T(8,128)(2,1)S(1)}, bf16[24,384]{1,0:T(8,128)(2,1)}, u32[]{:S(2)}) copy-start(bf16[24,384]{1,0:T(8,128)(2,1)} %constant.38.clone.c_ref) | copy-start | bytes 55300
  2.9 3.9 %copy-start.1 = (f32[32,64,512]{2,1,0:T(8,128)S(1)}, f32[32,64,512]{2,1,0:T(8,128)}, u32[]{:S(2)}) copy-start(f32[32,64,512]{2,1,0:T(8,128)} %u_ref.3) | copy-start | bytes 12582916
  2.9 4.0 %copy-start.10 = (bf16[2,112,240]{2,1,0:T(8,128)(2,1)S(1)}, bf16[2,112,240]{2,1,0:T(8,128)(2,1)}, u32[]{:S(2)}) copy-start(bf16[2,112,240]{2,1,0:T(8,128)(2,1)} %constant.39.clone.t_ref) | copy-start | bytes 322564
  4.5 2.4 %collective-permute-start = (f32[384,512]{1,0:T(8,128)S(1)}, f32[384,512]{1,0:T(8,128)S(1)}, u32[]{:S(2)}, u32[]{:S(2)}) collective-permute-start(f32[384,512]{1,0:T(8,128)S(1)} %x_send.1), channel_id=1, source_target_pairs={{0,16},{16,0},{1,17},{17,1},{2,18},{18,2},{3,19},{19,3},{4,20},{20... | collective-permute-start | bytes 2359304 | tf_op jit(solution)/shard_map/ppermute | solution.py:159
  9.5 7.3 %copy-start.2 = (bf16[1536,512]{1,0:T(8,128)(2,1)S(1)}, bf16[1536,512]{1,0:T(8,128)(2,1)}, u32[]{:S(2)}) copy-start(bf16[1536,512]{1,0:T(8,128)(2,1)} %constant.41.clone.m1) | copy-start | bytes 4718596
  9.5 7.3 %copy-start.3 = (bf16[1536,256]{1,0:T(8,128)(2,1)S(1)}, bf16[1536,256]{1,0:T(8,128)(2,1)}, u32[]{:S(2)}) copy-start(bf16[1536,256]{1,0:T(8,128)(2,1)} %constant.42.clone.m2) | copy-start | bytes 2359300
  9.5 7.3 %copy-start.5 = (bf16[1536,128]{1,0:T(8,128)(2,1)S(1)}, bf16[1536,128]{1,0:T(8,128)(2,1)}, u32[]{:S(2)}) copy-start(bf16[1536,128]{1,0:T(8,128)(2,1)} %constant.43.clone.m3) | copy-start | bytes 1179652
  9.5 7.3 %copy-start.7 = (bf16[256,512]{1,0:T(8,128)(2,1)S(1)}, bf16[256,512]{1,0:T(8,128)(2,1)}, u32[]{:S(2)}) copy-start(bf16[256,512]{1,0:T(8,128)(2,1)} %constant.44.clone.h1) | copy-start | bytes 786436
  9.5 7.3 %copy-start.8 = (bf16[256,256]{1,0:T(8,128)(2,1)S(1)}, bf16[256,256]{1,0:T(8,128)(2,1)}, u32[]{:S(2)}) copy-start(bf16[256,256]{1,0:T(8,128)(2,1)} %constant.45.clone.h2) | copy-start | bytes 393220
  9.6 7.3 %copy-start.9 = (f32[224,128]{1,0:T(8,128)S(1)}, f32[224,128]{1,0:T(8,128)}, u32[]{:S(2)}) copy-start(f32[224,128]{1,0:T(8,128)} %constant.49.clone.k3) | copy-start | bytes 344068
  9.6 7.3 %copy-start.11 = (bf16[256,128]{1,0:T(8,128)(2,1)S(1)}, bf16[256,128]{1,0:T(8,128)(2,1)}, u32[]{:S(2)}) copy-start(bf16[256,128]{1,0:T(8,128)(2,1)} %constant.46.clone.h3) | copy-start | bytes 196612
  9.6 7.3 %copy-start.12 = (f32[96,128]{1,0:T(8,128)S(1)}, f32[96,128]{1,0:T(8,128)}, u32[]{:S(2)}) copy-start(f32[96,128]{1,0:T(8,128)} %constant.48.clone.k2) | copy-start | bytes 147460
  9.6 7.3 %copy-start.15 = (f32[32,128]{1,0:T(8,128)S(1)}, f32[32,128]{1,0:T(8,128)}, u32[]{:S(2)}) copy-start(f32[32,128]{1,0:T(8,128)} %constant.47.clone.k1) | copy-start | bytes 49156
  9.6 6.1 %collective-permute-start.1 = (f32[24,512]{1,0:T(8,128)S(1)}, f32[24,512]{1,0:T(8,128)S(1)}, u32[]{:S(2)}, u32[]{:S(2)}) collective-permute-start(f32[24,512]{1,0:T(8,128)S(1)} %get-tuple-element.18), channel_id=1, source_target_pairs={{0,4},{4,8},{8,12},{12,0},{1,5},{5,9},{9,13},{13,1},{2,6},{6,10},{... | collective-permute-start | bytes 147464 | tf_op jit(solution)/shard_map/ppermute | solution.py:651
  12.5 4.3 %collective-permute-start.2 = (f32[24,512]{1,0:T(8,128)S(1)}, f32[24,512]{1,0:T(8,128)S(1)}, u32[]{:S(2)}, u32[]{:S(2)}) collective-permute-start(f32[24,512]{1,0:T(8,128)S(1)} %get-tuple-element.19), channel_id=1, source_target_pairs={{4,0},{8,4},{12,8},{0,12},{5,1},{9,5},{13,9},{1,13},{6,2},{10,6},{... | collective-permute-start | bytes 147464 | tf_op jit(solution)/shard_map/ppermute | solution.py:651
  13.6 8.4 %copy-start.16 = (bf16[1536,512]{1,0:T(8,128)(2,1)S(1)}, bf16[1536,512]{1,0:T(8,128)(2,1)}, u32[]{:S(2)}) copy-start(bf16[1536,512]{1,0:T(8,128)(2,1)} %constant.50.clone.m2) | copy-start | bytes 4718596
  13.6 8.4 %copy-start.17 = (bf16[1536,512]{1,0:T(8,128)(2,1)S(1)}, bf16[1536,512]{1,0:T(8,128)(2,1)}, u32[]{:S(2)}) copy-start(bf16[1536,512]{1,0:T(8,128)(2,1)} %constant.51.clone.m3) | copy-start | bytes 4718596
  13.6 8.4 %copy-start.18 = (bf16[4,256,512]{2,1,0:T(8,128)(2,1)S(1)}, bf16[4,256,512]{2,1,0:T(8,128)(2,1)}, u32[]{:S(2)}) copy-start(bf16[4,256,512]{2,1,0:T(8,128)(2,1)} %constant.52.clone.h1) | copy-start | bytes 3145732
  13.6 8.4 %copy-start.19 = (bf16[2,256,512]{2,1,0:T(8,128)(2,1)S(1)}, bf16[2,256,512]{2,1,0:T(8,128)(2,1)}, u32[]{:S(2)}) copy-start(bf16[2,256,512]{2,1,0:T(8,128)(2,1)} %constant.53.clone.h2) | copy-start | bytes 1572868
  13.6 8.4 %copy-start.20 = (bf16[1,256,512]{2,1,0:T(8,128)(2,1)S(1)}, bf16[1,256,512]{2,1,0:T(8,128)(2,1)}, u32[]{:S(2)}) copy-start(bf16[1,256,512]{2,1,0:T(8,128)(2,1)} %constant.54.clone.h3) | copy-start | bytes 786436
  18.0 16.8 %collective-permute-start.3 = (f32[192,512]{1,0:T(8,128)S(1)}, f32[192,512]{1,0:T(8,128)S(1)}, u32[]{:S(2)}, u32[]{:S(2)}) collective-permute-start(f32[192,512]{1,0:T(8,128)S(1)} %get-tuple-element.23), channel_id=1, source_target_pairs={{0,1},{1,2},{2,3},{3,0},{4,5},{5,6},{6,7},{7,4},{8,9},{9,10},{10,1... | collective-permute-start | bytes 1179656 | tf_op jit(solution)/shard_map/ppermute | solution.py:651
  19.7 18.5 %copy-start.4 = (bf16[512,512]{1,0:T(8,128)(2,1)S(1)}, bf16[512,512]{1,0:T(8,128)(2,1)}, u32[]{:S(2)}) copy-start(bf16[512,512]{1,0:T(8,128)(2,1)} %constant.55.clone.t2) | copy-start | bytes 1572868
  19.7 18.5 %copy-start.6 = (bf16[256,512]{1,0:T(8,128)(2,1)S(1)}, bf16[256,512]{1,0:T(8,128)(2,1)}, u32[]{:S(2)}) copy-start(bf16[256,512]{1,0:T(8,128)(2,1)} %constant.56.clone.t3) | copy-start | bytes 786436
  19.7 18.4 %collective-permute-start.4 = (f32[192,512]{1,0:T(8,128)S(1)}, f32[192,512]{1,0:T(8,128)S(1)}, u32[]{:S(2)}, u32[]{:S(2)}) collective-permute-start(f32[192,512]{1,0:T(8,128)S(1)} %get-tuple-element.24), channel_id=1, source_target_pairs={{1,0},{2,1},{3,2},{0,3},{5,4},{6,5},{7,6},{4,7},{9,8},{10,9},{11,1... | collective-permute-start | bytes 1179656 | tf_op jit(solution)/shard_map/ppermute | solution.py:651
where the time goes:
time: 54.6 us; the launch traced here: 54.4 us
  Pallas kernels  36.6 us (67%)
  starting transfers between devices  8.32 us (15%)
  waiting for transfers between devices  6.28 us (12%)
  local copies, waits for them, and re-layouts  3.03 us (6%)
    pallas_call x1, Pallas kernels, z_apply(): pl.pallas_call(kernel, grid=(nz // step,), in_specs=[pl.BlockSpec((groups...  16.3 us
    pallas_call x1, Pallas kernels, main_part(): pl.pallas_call(kernel, in_specs=[VM] * 11, out_specs=VM, out_shape=vmem((...  12.9 us
    ppermute x2, starting transfers between devices, swap(): lax.ppermute(to_right, axis, right)  4.56 us
    ppermute x2, waiting for transfers between devices, swap(): lax.ppermute(to_left, axis, left)  4.36 us
    ppermute x2, starting transfers between devices, swap(): lax.ppermute(to_left, axis, left)  3.27 us
    unnamed x42, local copies, waits for them, and re-layouts  3.03 us
    pallas_call x1, Pallas kernels, x_apply(): pl.pallas_call(kernel, grid=(steps,), in_specs=[pl.BlockSpec((step, nx, n...  2.61 us
    pallas_call x1, Pallas kernels, z_combine(): pl.pallas_call(kernel, in_specs=[VM] * 3, out_specs=[VM] * 3, out_shape=[...  2.15 us
  transfers between devices with their start and end apart: 5, of which 3 were waited for; matrix products, arithmetic and copies ran while one was open for 0% of the time, Pallas kernels for 28%

commit v1 on v0

--- a/solution.py
+++ b/solution.py
@@ -113,6 +113,11 @@
 
 
 VM = pl.BlockSpec(memory_space=pltpu.VMEM)
+HB = pl.BlockSpec(memory_space=pltpu.HBM)
+
+
+def in_hbm(array):
+    return pltpu.with_memory_space_constraint(array, pltpu.HBM)
 
 
 def vmem(shape, dtype=F32):
@@ -130,26 +135,44 @@
     pair = np.zeros((24, 6 * nx), one.dtype)
     pair[:12, : 3 * nx] = one
     pair[12:, 3 * nx :] = one
-    step = 8
-
-    def kernel(u_ref, c_ref, out_ref):
+    step = 4
+    steps = nz // step
+
+    def kernel(u_hbm, c_hbm, u_ref, out_ref, c_ref, u_sem, c_sem):
+        table_copy = pltpu.make_async_copy(c_hbm, c_ref, c_sem)
+        copies = [
+            pltpu.make_async_copy(
+                u_hbm.at[i * step : i * step + step], u_ref.at[i * step : i * step + step], u_sem.at[i]
+            )
+            for i in range(steps)
+        ]
+        table_copy.start()
+        for copy in copies:
+            copy.start()
+        table_copy.wait()
         table = c_ref[...]
-        for p in range(step // 2):
-            parts = []
-            for z in (2 * p, 2 * p + 1):
-                hi, lo = split(u_ref[z])
-                parts += [hi, hi, lo]
-            out_ref[24 * p : 24 * p + 24, :] = dot(table, jnp.concatenate(parts, axis=0))
+        for i, copy in enumerate(copies):
+            copy.wait()
+            for p in range(i * step // 2, (i + 1) * step // 2):
+                parts = []
+                for z in (2 * p, 2 * p + 1):
+                    hi, lo = split(u_ref[z])
+                    parts += [hi, hi, lo]
+                out_ref[24 * p : 24 * p + 24, :] = dot(table, jnp.concatenate(parts, axis=0))
 
     return pl.pallas_call(
         kernel,
-        grid=(nz // step,),
-        in_specs=[pl.BlockSpec((step, nx, ny), lambda i: (i, 0, 0)), VM],
-        out_specs=pl.BlockSpec((12 * step, ny), lambda i: (i, 0)),
-        out_shape=jax.ShapeDtypeStruct((nz * 12, ny), F32),
+        in_specs=[HB, HB],
+        out_specs=[VM, VM],
+        out_shape=[vmem((nz, nx, ny)), vmem((nz * 12, ny))],
+        scratch_shapes=[
+            pltpu.VMEM(pair.shape, BF),
+            pltpu.SemaphoreType.DMA((steps,)),
+            pltpu.SemaphoreType.DMA,
+        ],
         compiler_params=params(16),
         name="x_send",
-    )(field, jnp.asarray(pair))
+    )(in_hbm(field), in_hbm(jnp.asarray(pair)))
 
 
 def x_exchange(message):
@@ -196,7 +219,7 @@
         lanes = lax.broadcasted_iota(jnp.int32, (rows, 128), 1)
         for z in range(step):
             start = pl.multiple_of(i * (12 * step) + 24 * (z // 2) + 8 * (z % 2), 8)
-            hi, lo = split(u_ref[z])
+            hi, lo = split(u_ref[i * step + z])
             rhi, rlo = split(r_ref[pl.ds(start, 16), :])
             stacked = jnp.concatenate([hi, rhi, hi, rhi, lo, rlo], axis=0)
             got = dot(t_ref[z % 2], stacked)
@@ -229,7 +252,7 @@
     return pl.pallas_call(
         kernel,
         grid=(steps,),
-        in_specs=[pl.BlockSpec((step, nx, ny), lambda i: (i, 0, 0)), VM, VM, VM],
+        in_specs=[VM] * 4,
         out_specs=[VM] * 5,
         out_shape=[vmem((nz * n, ny)) for n in counts] + [jax.ShapeDtypeStruct((24, 512), F32)] * 2,
         scratch_shapes=[pltpu.VMEM((nz * n, 384), BF) for n in counts],
@@ -440,8 +463,15 @@
     return out
 
 
+def touched_layers(nz):
+    one, two, three = [np.abs(p).max(axis=1) > 1e-12 for _, p in z_tables(nz)]
+    hit = lambda z: one[z] or (z % 2 == 0 and two[z // 2]) or (z % 4 == 0 and three[z // 4])
+    return [z for z in range(nz) if hit(z)]
+
+
 def main_part(xs, from_left, from_right, nz):
     ny = xs[0].shape[1]
+    untouched = [z for z in range(nz) if z not in touched_layers(nz)]
     counts = [x.shape[0] // nz for x in xs]
     mains, halos = [], []
     for level, (main, left, right) in enumerate(y_tables(ny, True)):
@@ -451,7 +481,7 @@
             np.stack([halo_table(left, right, level, [c], nz, counts) for c in range(chunks)])
         )
 
-    def kernel(x1, x2, x3, fl, fr, m1, m2, m3, h1, h2, h3, out_ref, y1, y2, y3, w2, halo_ref):
+    def kernel(x1, x2, x3, fl, fr, m1, m2, m3, h1, h2, h3, out_ref, hbm, y1, y2, y3, w2, halo_ref, sem):
         halo = turned(fl, fr).astype(BF)
         halo_ref[...] = jnp.concatenate([halo, halo], axis=1)
         for x, m, h, y, n in zip((x1, x2, x3), (m1, m2, m3), (h1, h2, h3), (y1, y2, y3), counts):
@@ -525,13 +555,25 @@
 
         lax.fori_loop(0, (counts[1] // 8) * groups, merge, 0)
 
+        copies = [
+            pltpu.make_async_copy(
+                out_ref.at[q, z], hbm.at[z, :, 128 * q : 128 * q + 128], sem.at[z]
+            )
+            for z in untouched
+            for q in range(groups)
+        ]
+        for copy in copies:
+            copy.start()
+        for copy in copies:
+            copy.wait()
+
     return pl.pallas_call(
         kernel,
         in_specs=[VM] * 11,
-        out_specs=VM,
-        out_shape=vmem((ny // 128, nz, counts[0], 128)),
+        out_specs=[VM, HB],
+        out_shape=[vmem((ny // 128, nz, counts[0], 128)), pltpu.HBM((nz, counts[0], ny), F32)],
         scratch_shapes=[pltpu.VMEM((nz * n, ny), F32) for n in counts]
-        + [pltpu.VMEM((ny // 128, nz // 2 * counts[1], 128), F32), pltpu.VMEM((512, 256), BF)],
+        + [pltpu.VMEM((ny // 128, nz // 2 * counts[1], 128), F32), pltpu.VMEM((512, 256), BF), pltpu.SemaphoreType.DMA((nz,))],
         compiler_params=params(32),
         cost_estimate=pl.CostEstimate(
             flops=8_000_000_000, bytes_accessed=20_000_000, transcendentals=0
@@ -540,7 +582,7 @@
     )(*xs, from_left, from_right, *[jnp.asarray(t) for t in mains], *[jnp.asarray(t) for t in halos])
 
 
-def z_apply(inner, from_left, from_right):
+def z_apply(inner, partial, from_left, from_right):
     groups, nz, nx, _ = inner.shape
     ny = groups * 128
     maps = [p for _, p in z_tables(nz)]
@@ -551,97 +593,101 @@
         hi = spread_columns(np.eye(width), 1 << level, ny).astype(ml_dtypes.bfloat16)
         tables.append(np.concatenate([hi, hi]))
     heights = [2 * counts[0], 3 * counts[1] // 2, 4 * counts[2] // 4]
-    step = 4
-
-    def kernel(in_ref, fl, fr, t2, t3, out_ref, s1, s2, s3):
-        i = pl.program_id(0)
-
-        @pl.when(i == 0)
-        def _():
-            row_ids = lax.broadcasted_iota(jnp.int32, (nx, ny), 0)
-            lane_ids = lax.broadcasted_iota(jnp.int32, (nx, ny), 1)
-            inside = ((row_ids % 2) + (lane_ids % 2)) == 0
-            s2[...] = jnp.zeros(s2.shape, F32)
-            s3[...] = jnp.zeros(s3.shape, F32)
-            for side, ref in enumerate((fl, fr)):
-                ranks = LEFT_RANKS if side == 0 else RIGHT_RANKS
-                for c in range(2):
-                    outside = jnp.where(inside, 0.0, ref[c * nx : c * nx + nx, :])
+    touched = touched_layers(nz)
+
+    def kernel(in_ref, base_hbm, fl, fr, t2, t3, out_hbm, s1, s2, s3, buf, sem):
+        del base_hbm
+        s3[...] = jnp.zeros(s3.shape, F32)
+        for side, ref in enumerate((fl, fr)):
+            for c in range(2):
+                for q in range(groups):
+                    s1[2 * side + c, q] = ref[c * nx : c * nx + nx, 128 * q : 128 * q + 128]
+            ranks = LEFT_RANKS if side == 0 else RIGHT_RANKS
+            at = heights[0]
+            for level, table, to in ((1, t2, s2), (2, t3, s3)):
+                width, tall, n = ny >> level, heights[level], counts[level]
+                flat = jnp.concatenate(
+                    [ref[at : at + tall, p * width : p * width + width] for p in range(1 << level)],
+                    axis=0,
+                )
+                hi, lo = split(flat)
+                got = dot(jnp.concatenate([hi, lo], axis=1), table[...])
+                first = 0 if side == 0 else LEFT_RANKS[level]
+                for c in range(ranks[level]):
                     for q in range(groups):
-                        s1[2 * side + c, q] = outside[:, 128 * q : 128 * q + 128]
-                at = heights[0]
-                for level, table, to in ((1, t2, s2), (2, t3, s3)):
-                    width, tall, n = ny >> level, heights[level], counts[level]
-                    flat = jnp.concatenate(
-                        [ref[at : at + tall, p * width : p * width + width] for p in range(1 << level)],
-                        axis=0,
-                    )
-                    hi, lo = split(flat)
-                    got = dot(jnp.concatenate([hi, lo], axis=1), table[...])
-                    first = 0 if side == 0 else LEFT_RANKS[level]
-                    for c in range(ranks[level]):
-                        for q in range(groups):
-                            to[first + c, q, pl.ds(0, n, stride=1 << level), :] = got[
-                                c * n : c * n + n, 128 * q : 128 * q + 128
-                            ]
-                    at += tall
-
-        for z_out in range(nz):
-
-            @pl.when(i == z_out // step)
-            def _(z=z_out):
-                def body(k, _):
-                    q = k % groups
-                    row = pl.multiple_of((k // groups) * 8, 8)
-                    lane = pl.multiple_of(q * 128, 128)
-                    value = in_ref[q, z % step, pl.ds(row, 8), :]
-                    extra = None
-                    for c in range(4):
-                        scalar = maps[0][z, c]
-                        if abs(scalar) < 1e-12:
-                            continue
-                        if z % 2:
-                            start = pl.multiple_of((c % 2) * nx + row, 8)
-                            term = (fl, fr)[c // 2][pl.ds(start, 8), pl.ds(lane, 128)]
+                        piece = got[c * n : c * n + n, 128 * q : 128 * q + 128]
+                        if level == 1:
+                            to[first + c, q] = piece
                         else:
-                            term = s1[c, q, pl.ds(row, 8), :]
-                        extra = add(extra, term * np.float32(scalar))
-                    if z % 2 == 0:
-                        for c in range(maps[1].shape[1]):
-                            scalar = maps[1][z // 2, c]
-                            if abs(scalar) > 1e-12:
-                                extra = add(extra, s2[c, q, pl.ds(row, 8), :] * np.float32(scalar))
+                            to[first + c, q, pl.ds(0, n, stride=2), :] = piece
+                at += tall
+
+        lanes = lax.broadcasted_iota(jnp.int32, (8, 128), 1)
+        even_lane = lanes % 2 == 0
+        third_cell = (lax.broadcasted_iota(jnp.int32, (8, 128), 0) % 2 + lanes % 4) == 0
+
+        def summed(table_row, get):
+            total = None
+            for c, scalar in enumerate(table_row):
+                if abs(scalar) > 1e-12:
+                    total = add(total, get(c) * np.float32(scalar))
+            return total
+
+        copies = []
+        for slot, z in enumerate(touched):
+
+            def body(t, _, z=z, slot=slot):
+                full = pl.multiple_of(16 * t, 8)
+                half = pl.multiple_of(8 * t, 8)
+                for q in range(groups):
+                    if z % 2:
+                        for more in (0, 8):
+                            rows = pl.ds(full + more, 8)
+                            extra = summed(maps[0][z], lambda c: s1[c, q, rows, :])
+                            buf[slot, q, rows, :] = add(in_ref[q, z, rows, :], extra)
+                        continue
+                    evens = pl.ds(16 * t, 8, stride=2)
+                    odds = pl.ds(16 * t + 1, 8, stride=2)
+                    extra = summed(maps[0][z], lambda c: s1[c, q, odds, :])
+                    buf[slot, q, odds, :] = add(in_ref[q, z, odds, :], extra)
+                    rows = pl.ds(half, 8)
+                    extra = summed(maps[1][z // 2], lambda c: s2[c, q, rows, :])
                     if z % 4 == 0:
-                        ids = (
-                            lax.broadcasted_iota(jnp.int32, (8, 128), 0) % 4
-                            + lax.broadcasted_iota(jnp.int32, (8, 128), 1) % 4
-                        )
-                        third = None
-                        for c in range(maps[2].shape[1]):
-                            if abs(maps[2][z // 4, c]) > 1e-12:
-                                third = add(third, s3[c, q, pl.ds(row, 8), :] * np.float32(maps[2][z // 4, c]))
-                        if third is None:
-                            third = jnp.zeros((8, 128), F32)
-                        if extra is None:
-                            extra = jnp.zeros((8, 128), F32)
-                        extra = jnp.where(ids == 0, third, extra)
-                    if extra is not None:
-                        value = value + extra
-                    out_ref[z % step, pl.ds(row, 8), pl.ds(lane, 128)] = value
-                    return 0
-
-                lax.fori_loop(0, (nx // 8) * groups, body, 0)
+                        third = summed(maps[2][z // 4], lambda c: s3[c, q, rows, :])
+                        third = 0.0 if third is None else third
+                        extra = jnp.where(third_cell, third, 0.0 if extra is None else extra)
+                    one = summed(maps[0][z], lambda c: s1[c, q, evens, :])
+                    if one is not None:
+                        extra = jnp.where(even_lane, 0.0 if extra is None else extra, one)
+                    buf[slot, q, evens, :] = add(in_ref[q, z, evens, :], extra)
+                return 0
+
+            lax.fori_loop(0, nx // 16, body, 0)
+            for q in range(groups):
+                copy = pltpu.make_async_copy(
+                    buf.at[slot, q], out_hbm.at[z, :, 128 * q : 128 * q + 128], sem.at[slot]
+                )
+                copy.start()
+                copies.append(copy)
+        for copy in copies:
+            copy.wait()
 
     return pl.pallas_call(
         kernel,
-        grid=(nz // step,),
-        in_specs=[pl.BlockSpec((groups, step, nx, 128), lambda i: (0, i, 0, 0)), VM, VM, VM, VM],
-        out_specs=pl.BlockSpec((step, nx, ny), lambda i: (i, 0, 0)),
+        in_specs=[VM, HB, VM, VM, VM, VM],
+        out_specs=HB,
         out_shape=jax.ShapeDtypeStruct((nz, nx, ny), F32),
-        scratch_shapes=[pltpu.VMEM((m.shape[1], groups, nx, 128), F32) for m in maps],
+        input_output_aliases={1: 0},
+        scratch_shapes=[
+            pltpu.VMEM((4, groups, nx, 128), F32),
+            pltpu.VMEM((maps[1].shape[1], groups, nx // 2, 128), F32),
+            pltpu.VMEM((maps[2].shape[1], groups, nx // 2, 128), F32),
+            pltpu.VMEM((len(touched), groups, nx, 128), F32),
+            pltpu.SemaphoreType.DMA((len(touched),)),
+        ],
         compiler_params=params(24),
         name="z_apply",
-    )(inner, from_left, from_right, *[jnp.asarray(t) for t in tables])
+    )(inner, partial, from_left, from_right, *[jnp.asarray(t) for t in tables])
 
 
 def swap(to_right, to_left, axis):
@@ -653,14 +699,15 @@
 
 def local(field):
     nz = field.shape[0]
-    halo = x_exchange(x_send(field))
+    field, message = x_send(field)
+    halo = x_exchange(message)
     x1, x2, x3, to_right, to_left = x_apply(field, halo)
     from_left, from_right = swap(to_right, to_left, "gy")
     combined = z_combine((x1, x2, x3), nz)
     to_right, to_left = y_messages(combined, from_left, from_right, nz)
     below, above = swap(to_right, to_left, "gz")
-    inner = main_part((x1, x2, x3), from_left, from_right, nz)
-    return z_apply(inner, below, above)
+    inner, partial = main_part((x1, x2, x3), from_left, from_right, nz)
+    return z_apply(inner, partial, below, above)
 
 
 def solution(mesh):

time: 54.6 us -> 40.3 us (0.74)
  Pallas kernels: 36.6 us -> 26.8 us
  local copies, waits for them, and re-layouts: 3.03 us -> 0.11 us
  waiting for transfers between devices: 6.28 us -> 4.77 us
    pallas_call x4, Pallas kernels: 33.3 us -> 23.5 us  [the longest x1 14.4 us: main_part(): pl.pallas_call(kernel, in_specs=[VM] * 11, out_specs=[VM, HB], out_shape=...]
    unnamed x42 -> x36, local copies, waits for them, and re-layouts: 3.03 us -> 0.11 us
    ppermute x2, waiting for transfers between devices: 4.36 us -> 2.85 us  [swap(): lax.ppermute(to_left, axis, left)]
  transfers between devices with their start and end apart: 5 -> 5, of which waited for: 3 -> 3; matrix products, arithmetic and copies ran while one was open for 0% -> 0% of each run, Pallas kernels for 28% -> 41%
where the time goes in v1:
time: 40.3 us; the launch traced here: 40.2 us
  Pallas kernels  26.8 us (67%)
  starting transfers between devices  8.32 us (21%)
  waiting for transfers between devices  4.77 us (12%)
    pallas_call x1, Pallas kernels, main_part(): pl.pallas_call(kernel, in_specs=[VM] * 11, out_specs=[VM, HB], out_shape=...  14.4 us
    ppermute x2, starting transfers between devices, swap(): lax.ppermute(to_right, axis, right)  4.54 us
    pallas_call x1, Pallas kernels, x_send(): pl.pallas_call(kernel, in_specs=[HB, HB], out_specs=[VM, VM], out_shape=[...  3.96 us
    ppermute x2, starting transfers between devices, swap(): lax.ppermute(to_left, axis, left)  3.27 us
    ppermute x2, waiting for transfers between devices, swap(): lax.ppermute(to_left, axis, left)  2.85 us
    pallas_call x1, Pallas kernels, x_apply(): pl.pallas_call(kernel, grid=(steps,), in_specs=[VM] * 4, out_specs=[VM] *...  2.6 us
    pallas_call x1, Pallas kernels, z_apply(): pl.pallas_call(kernel, in_specs=[VM, HB, VM, VM, VM, VM], out_specs=HB, o...  2.53 us
    pallas_call x1, Pallas kernels, z_combine(): pl.pallas_call(kernel, in_specs=[VM] * 3, out_specs=[VM] * 3, out_shape=[...  2.15 us
  transfers between devices with their start and end apart: 5, of which 3 were waited for; matrix products, arithmetic and copies ran while one was open for 0% of the time, Pallas kernels for 41%

profile of v1, /device:TPU:0, one launch (start us, length us, event | category | flops | bytes accessed | tf_op | source)
XLA Modules:
  0.0 40.2 jit_solution(7043703908756976457)
XLA Ops:
  0.0 0.0 copy-start.11
  0.0 0.0 copy-start.8
  0.0 4.0 %x_send.1 = (f32[32,64,512]{2,1,0:T(8,128)S(1)}, f32[384,512]{1,0:T(8,128)S(1)}) custom-call(f32[32,64,512]{2,1,0:T(8,128)} %u_hbm.1, bf16[24,384]{1,0:T(8,128)(2,1)} %constant.38.clone.c_hbm), custom_call_target="tpu_custom_call" | custom-call | tf_op jit(solution)/shard_map/x_send/pallas_call | solution.py:163
  4.0 0.5 %collective-permute-start = (f32[384,512]{1,0:T(8,128)S(1)}, f32[384,512]{1,0:T(8,128)S(1)}, u32[]{:S(2)}, u32[]{:S(2)}) collective-permute-start(f32[384,512]{1,0:T(8,128)S(1)} %get-tuple-element.20), channel_id=1, source_target_pairs={{0,16},{16,0},{1,17},{17,1},{2,18},{18,2},{3,19},{19,3},{4,20},{20... | collective-permute-start | bytes 2359304 | tf_op jit(solution)/shard_map/ppermute | solution.py:182
  4.5 1.9 %collective-permute-done.r_ref = f32[384,512]{1,0:T(8,128)S(1)} collective-permute-done((f32[384,512]{1,0:T(8,128)S(1)}, f32[384,512]{1,0:T(8,128)S(1)}, u32[]{:S(2)}, u32[]{:S(2)}) %collective-permute-start) | collective-permute-done | bytes 786464 | tf_op jit(solution)/shard_map/ppermute | solution.py:182
  6.4 0.0 copy-done.11
  6.4 0.0 copy-done.8
  6.4 2.6 %x_apply.1 = (f32[2048,512]{1,0:T(8,128)S(1)}, f32[1024,512]{1,0:T(8,128)S(1)}, f32[512,512]{1,0:T(8,128)S(1)}, f32[24,512]{1,0:T(8,128)S(1)}, f32[24,512]{1,0:T(8,128)S(1)}) custom-call(f32[32,64,512]{2,1,0:T(8,128)S(1)} %get-tuple-element.19.u_ref, f32[384,512]{1,0:T(8,128)S(1)} %collective-permute-done.r_ref, bf16[2,112,240]{2,1,0:T(8,128)(2,1)S(1)} %copy-done.8, ...), custom_call_target="tpu_custom_call" | custom-call | tf_op jit(solution)/shard_map/x_apply/pallas_call | solution.py:252
  9.0 0.0 copy-start.1
  9.0 0.0 copy-start.3
  9.0 0.0 copy-start.5
  9.1 0.0 copy-start.6
  9.1 0.0 copy-start.7
  9.1 0.0 copy-start.9
  9.1 0.0 copy-start.10
  9.1 0.0 copy-start.12
  9.1 2.9 %collective-permute-start.1 = (f32[24,512]{1,0:T(8,128)S(1)}, f32[24,512]{1,0:T(8,128)S(1)}, u32[]{:S(2)}, u32[]{:S(2)}) collective-permute-start(f32[24,512]{1,0:T(8,128)S(1)} %get-tuple-element.24), channel_id=1, source_target_pairs={{0,4},{4,8},{8,12},{12,0},{1,5},{5,9},{9,13},{13,1},{2,6},{6,10},{... | collective-permute-start | bytes 147464 | tf_op jit(solution)/shard_map/ppermute | solution.py:697
  12.0 1.0 %collective-permute-start.2 = (f32[24,512]{1,0:T(8,128)S(1)}, f32[24,512]{1,0:T(8,128)S(1)}, u32[]{:S(2)}, u32[]{:S(2)}) collective-permute-start(f32[24,512]{1,0:T(8,128)S(1)} %get-tuple-element.25), channel_id=1, source_target_pairs={{4,0},{8,4},{12,8},{0,12},{5,1},{9,5},{13,9},{1,13},{6,2},{10,6},{... | collective-permute-start | bytes 147464 | tf_op jit(solution)/shard_map/ppermute | solution.py:697
  13.1 0.0 copy-start.13
  13.1 0.0 copy-start.14
  13.1 0.0 copy-start.15
  13.1 0.0 copy-start.17
  13.1 2.2 %z_combine.1 = (f32[256,512]{1,0:T(8,128)S(1)}, f32[192,512]{1,0:T(8,128)S(1)}, f32[112,512]{1,0:T(8,128)S(1)}) custom-call(f32[2048,512]{1,0:T(8,128)S(1)} %get-tuple-element.21.x1, f32[1024,512]{1,0:T(8,128)S(1)} %get-tuple-element.22.x2, f32[512,512]{1,0:T(8,128)S(1)} %get-tuple-element.23.x3), custom_call_target="tpu_custom_call" | custom-call | flops 20000000 | bytes 6000000 | tf_op jit(solution)/shard_map/z_combine/pallas_call | solution.py:304
  15.2 0.0 collective-permute-done.1.fl
  15.2 1.1 %collective-permute-done.2.fr = f32[24,512]{1,0:T(8,128)S(1)} collective-permute-done((f32[24,512]{1,0:T(8,128)S(1)}, f32[24,512]{1,0:T(8,128)S(1)}, u32[]{:S(2)}, u32[]{:S(2)}) %collective-permute-start.2) | collective-permute-done | bytes 49184 | tf_op jit(solution)/shard_map/ppermute | solution.py:697
  16.3 0.0 copy-done
  16.3 0.0 copy-done.1
  16.3 0.0 copy-done.3
  16.3 0.0 copy-done.5
  16.4 0.0 copy-done.6
  16.4 0.0 copy-done.7
  16.4 0.0 copy-done.9
  16.4 0.0 copy-done.10
  16.4 0.0 copy-done.12
  16.4 1.1 %y_messages.1 = (f32[192,512]{1,0:T(8,128)S(1)}, f32[192,512]{1,0:T(8,128)S(1)}) custom-call(f32[256,512]{1,0:T(8,128)S(1)} %get-tuple-element.28.c1, f32[192,512]{1,0:T(8,128)S(1)} %get-tuple-element.29.c2, f32[112,512]{1,0:T(8,128)S(1)} %get-tuple-element.30.c3, f32[24,512]{1,0:T(8,128)S(1)} %collective-permute-done.1.fl, ...), custom_call_target="tpu_custom_call" | custom-call | tf_op jit(solution)/shard_map/y_messages/pallas_call | solution.py:420
  17.5 1.6 %collective-permute-start.3 = (f32[192,512]{1,0:T(8,128)S(1)}, f32[192,512]{1,0:T(8,128)S(1)}, u32[]{:S(2)}, u32[]{:S(2)}) collective-permute-start(f32[192,512]{1,0:T(8,128)S(1)} %get-tuple-element.31), channel_id=1, source_target_pairs={{0,1},{1,2},{2,3},{3,0},{4,5},{5,6},{6,7},{7,4},{8,9},{9,10},{10,1... | collective-permute-start | bytes 1179656 | tf_op jit(solution)/shard_map/ppermute | solution.py:697
  19.2 2.2 %collective-permute-start.4 = (f32[192,512]{1,0:T(8,128)S(1)}, f32[192,512]{1,0:T(8,128)S(1)}, u32[]{:S(2)}, u32[]{:S(2)}) collective-permute-start(f32[192,512]{1,0:T(8,128)S(1)} %get-tuple-element.32), channel_id=1, source_target_pairs={{1,0},{2,1},{3,2},{0,3},{5,4},{6,5},{7,6},{4,7},{9,8},{10,9},{11,1... | collective-permute-start | bytes 1179656 | tf_op jit(solution)/shard_map/ppermute | solution.py:697
  21.4 0.0 copy-done.13
  21.4 0.0 copy-done.14
  21.4 0.0 copy-done.15
  21.4 0.0 copy-done.16
  21.4 0.0 copy-done.17
  21.5 14.4 %main_part.1 = (f32[4,32,64,128]{3,2,1,0:T(8,128)S(1)}, f32[32,64,512]{2,1,0:T(8,128)}) custom-call(f32[2048,512]{1,0:T(8,128)S(1)} %get-tuple-element.21.x1, f32[1024,512]{1,0:T(8,128)S(1)} %get-tuple-element.22.x2, f32[512,512]{1,0:T(8,128)S(1)} %get-tuple-element.23.x3, f32[24,512]{1,0:T(8,128)S(1)} %collective-permute-done.1.fl, ...), custom_call_target="tpu_custom_call" | custom-call | flops 8000000000 | bytes 20000000 | tf_op jit(solution)/shard_map/main_part/pallas_call | solution.py:570
  35.9 0.0 collective-permute-done.3.fl
  35.9 1.8 %collective-permute-done.4.fr = f32[192,512]{1,0:T(8,128)S(1)} collective-permute-done((f32[192,512]{1,0:T(8,128)S(1)}, f32[192,512]{1,0:T(8,128)S(1)}, u32[]{:S(2)}, u32[]{:S(2)}) %collective-permute-start.4) | collective-permute-done | bytes 393248 | tf_op jit(solution)/shard_map/ppermute | solution.py:697
  37.7 0.0 copy-done.2
  37.7 0.0 copy-done.4
  37.7 2.5 %z_apply.1 = f32[32,64,512]{2,1,0:T(8,128)} custom-call(f32[4,32,64,128]{3,2,1,0:T(8,128)S(1)} %get-tuple-element.26.in_ref, f32[32,64,512]{2,1,0:T(8,128)} %get-tuple-element.27.base_hbm, f32[192,512]{1,0:T(8,128)S(1)} %collective-permute-done.3.fl, f32[192,512]{1,0:T(8,128)S(1)} %collective-permute-done.4.fr, ...), custom_call_target="tpu_custom_call", output_to_operand_aliasing={{}: (1, {})} | custom-call | tf_op jit(solution)/shard_map/z_apply/pallas_call | solution.py:675
  (4 shorter events, 0.0 us)
Async XLA Ops:
  0.0 6.4 %copy-start.11 = (bf16[3,8,384]{2,1,0:T(8,128)(2,1)S(1)}, bf16[3,8,384]{2,1,0:T(8,128)(2,1)}, u32[]{:S(2)}) copy-start(bf16[3,8,384]{2,1,0:T(8,128)(2,1)} %constant.40.clone.c_ref) | copy-start | bytes 55300
  0.0 6.4 %copy-start.8 = (bf16[2,112,240]{2,1,0:T(8,128)(2,1)S(1)}, bf16[2,112,240]{2,1,0:T(8,128)(2,1)}, u32[]{:S(2)}) copy-start(bf16[2,112,240]{2,1,0:T(8,128)(2,1)} %constant.39.clone.t_ref) | copy-start | bytes 322564
  4.0 2.4 %collective-permute-start = (f32[384,512]{1,0:T(8,128)S(1)}, f32[384,512]{1,0:T(8,128)S(1)}, u32[]{:S(2)}, u32[]{:S(2)}) collective-permute-start(f32[384,512]{1,0:T(8,128)S(1)} %get-tuple-element.20), channel_id=1, source_target_pairs={{0,16},{16,0},{1,17},{17,1},{2,18},{18,2},{3,19},{19,3},{4,20},{20... | collective-permute-start | bytes 2359304 | tf_op jit(solution)/shard_map/ppermute | solution.py:182
  9.0 7.3 %copy-start = (bf16[1536,512]{1,0:T(8,128)(2,1)S(1)}, bf16[1536,512]{1,0:T(8,128)(2,1)}, u32[]{:S(2)}) copy-start(bf16[1536,512]{1,0:T(8,128)(2,1)} %constant.41.clone.m1) | copy-start | bytes 4718596
  9.0 7.3 %copy-start.1 = (bf16[1536,256]{1,0:T(8,128)(2,1)S(1)}, bf16[1536,256]{1,0:T(8,128)(2,1)}, u32[]{:S(2)}) copy-start(bf16[1536,256]{1,0:T(8,128)(2,1)} %constant.42.clone.m2) | copy-start | bytes 2359300
  9.0 7.3 %copy-start.3 = (bf16[1536,128]{1,0:T(8,128)(2,1)S(1)}, bf16[1536,128]{1,0:T(8,128)(2,1)}, u32[]{:S(2)}) copy-start(bf16[1536,128]{1,0:T(8,128)(2,1)} %constant.43.clone.m3) | copy-start | bytes 1179652
  9.0 7.3 %copy-start.5 = (bf16[256,512]{1,0:T(8,128)(2,1)S(1)}, bf16[256,512]{1,0:T(8,128)(2,1)}, u32[]{:S(2)}) copy-start(bf16[256,512]{1,0:T(8,128)(2,1)} %constant.44.clone.h1) | copy-start | bytes 786436
  9.1 7.3 %copy-start.6 = (bf16[256,256]{1,0:T(8,128)(2,1)S(1)}, bf16[256,256]{1,0:T(8,128)(2,1)}, u32[]{:S(2)}) copy-start(bf16[256,256]{1,0:T(8,128)(2,1)} %constant.45.clone.h2) | copy-start | bytes 393220
  9.1 7.3 %copy-start.7 = (f32[224,128]{1,0:T(8,128)S(1)}, f32[224,128]{1,0:T(8,128)}, u32[]{:S(2)}) copy-start(f32[224,128]{1,0:T(8,128)} %constant.49.clone.k3) | copy-start | bytes 344068
  9.1 7.3 %copy-start.9 = (bf16[256,128]{1,0:T(8,128)(2,1)S(1)}, bf16[256,128]{1,0:T(8,128)(2,1)}, u32[]{:S(2)}) copy-start(bf16[256,128]{1,0:T(8,128)(2,1)} %constant.46.clone.h3) | copy-start | bytes 196612
  9.1 7.3 %copy-start.10 = (f32[96,128]{1,0:T(8,128)S(1)}, f32[96,128]{1,0:T(8,128)}, u32[]{:S(2)}) copy-start(f32[96,128]{1,0:T(8,128)} %constant.48.clone.k2) | copy-start | bytes 147460
  9.1 7.3 %copy-start.12 = (f32[32,128]{1,0:T(8,128)S(1)}, f32[32,128]{1,0:T(8,128)}, u32[]{:S(2)}) copy-start(f32[32,128]{1,0:T(8,128)} %constant.47.clone.k1) | copy-start | bytes 49156
  9.1 6.1 %collective-permute-start.1 = (f32[24,512]{1,0:T(8,128)S(1)}, f32[24,512]{1,0:T(8,128)S(1)}, u32[]{:S(2)}, u32[]{:S(2)}) collective-permute-start(f32[24,512]{1,0:T(8,128)S(1)} %get-tuple-element.24), channel_id=1, source_target_pairs={{0,4},{4,8},{8,12},{12,0},{1,5},{5,9},{9,13},{13,1},{2,6},{6,10},{... | collective-permute-start | bytes 147464 | tf_op jit(solution)/shard_map/ppermute | solution.py:697
  12.0 4.3 %collective-permute-start.2 = (f32[24,512]{1,0:T(8,128)S(1)}, f32[24,512]{1,0:T(8,128)S(1)}, u32[]{:S(2)}, u32[]{:S(2)}) collective-permute-start(f32[24,512]{1,0:T(8,128)S(1)} %get-tuple-element.25), channel_id=1, source_target_pairs={{4,0},{8,4},{12,8},{0,12},{5,1},{9,5},{13,9},{1,13},{6,2},{10,6},{... | collective-permute-start | bytes 147464 | tf_op jit(solution)/shard_map/ppermute | solution.py:697
  13.1 8.4 %copy-start.13 = (bf16[1536,512]{1,0:T(8,128)(2,1)S(1)}, bf16[1536,512]{1,0:T(8,128)(2,1)}, u32[]{:S(2)}) copy-start(bf16[1536,512]{1,0:T(8,128)(2,1)} %constant.51.clone.m3) | copy-start | bytes 4718596
  13.1 8.4 %copy-start.14 = (bf16[1536,512]{1,0:T(8,128)(2,1)S(1)}, bf16[1536,512]{1,0:T(8,128)(2,1)}, u32[]{:S(2)}) copy-start(bf16[1536,512]{1,0:T(8,128)(2,1)} %constant.50.clone.m2) | copy-start | bytes 4718596
  13.1 8.4 %copy-start.15 = (bf16[4,256,512]{2,1,0:T(8,128)(2,1)S(1)}, bf16[4,256,512]{2,1,0:T(8,128)(2,1)}, u32[]{:S(2)}) copy-start(bf16[4,256,512]{2,1,0:T(8,128)(2,1)} %constant.52.clone.h1) | copy-start | bytes 3145732
  13.1 8.4 %copy-start.16 = (bf16[2,256,512]{2,1,0:T(8,128)(2,1)S(1)}, bf16[2,256,512]{2,1,0:T(8,128)(2,1)}, u32[]{:S(2)}) copy-start(bf16[2,256,512]{2,1,0:T(8,128)(2,1)} %constant.53.clone.h2) | copy-start | bytes 1572868
  13.1 8.4 %copy-start.17 = (bf16[1,256,512]{2,1,0:T(8,128)(2,1)S(1)}, bf16[1,256,512]{2,1,0:T(8,128)(2,1)}, u32[]{:S(2)}) copy-start(bf16[1,256,512]{2,1,0:T(8,128)(2,1)} %constant.54.clone.h3) | copy-start | bytes 786436
  17.5 18.3 %collective-permute-start.3 = (f32[192,512]{1,0:T(8,128)S(1)}, f32[192,512]{1,0:T(8,128)S(1)}, u32[]{:S(2)}, u32[]{:S(2)}) collective-permute-start(f32[192,512]{1,0:T(8,128)S(1)} %get-tuple-element.31), channel_id=1, source_target_pairs={{0,1},{1,2},{2,3},{3,0},{4,5},{5,6},{6,7},{7,4},{8,9},{9,10},{10,1... | collective-permute-start | bytes 1179656 | tf_op jit(solution)/shard_map/ppermute | solution.py:697
  19.2 18.5 %copy-start.2 = (bf16[512,512]{1,0:T(8,128)(2,1)S(1)}, bf16[512,512]{1,0:T(8,128)(2,1)}, u32[]{:S(2)}) copy-start(bf16[512,512]{1,0:T(8,128)(2,1)} %constant.55.clone.t2) | copy-start | bytes 1572868
  19.2 18.5 %copy-start.4 = (bf16[256,512]{1,0:T(8,128)(2,1)S(1)}, bf16[256,512]{1,0:T(8,128)(2,1)}, u32[]{:S(2)}) copy-start(bf16[256,512]{1,0:T(8,128)(2,1)} %constant.56.clone.t3) | copy-start | bytes 786436
  19.2 18.5 %collective-permute-start.4 = (f32[192,512]{1,0:T(8,128)S(1)}, f32[192,512]{1,0:T(8,128)S(1)}, u32[]{:S(2)}, u32[]{:S(2)}) collective-permute-start(f32[192,512]{1,0:T(8,128)S(1)} %get-tuple-element.32), channel_id=1, source_target_pairs={{1,0},{2,1},{3,2},{0,3},{5,4},{6,5},{7,6},{4,7},{9,8},{10,9},{11,1... | collective-permute-start | bytes 1179656 | tf_op jit(solution)/shard_map/ppermute | solution.py:697

commit v2 on v1

--- a/solution.py
+++ b/solution.py
@@ -67,11 +67,18 @@
     return out
 
 
+def nested_space(outer):
+    first = row_space(outer[0], 2)
+    every = np.concatenate(outer)
+    rest = every - every @ first.T @ first
+    return np.concatenate([first, row_space(rest, 4)])
+
+
 @functools.lru_cache(None)
 def joint_sides(n):
     found = blocks(n)
-    cl = row_space(np.concatenate([b[1] for b in found]), 6)
-    cr = row_space(np.concatenate([b[2] for b in found]), 6)
+    cl = nested_space([b[1] for b in found])
+    cr = nested_space([b[2] for b in found])
     maps = [(b[0], b[1] @ cl.T, b[2] @ cr.T) for b in found]
     return cl, cr, maps
 
@@ -137,8 +144,12 @@
     pair[12:, 3 * nx :] = one
     step = 4
     steps = nz // step
-
-    def kernel(u_hbm, c_hbm, u_ref, out_ref, c_ref, u_sem, c_sem):
+    order = [0, steps - 1] + list(range(1, steps - 1))
+    flight = 3
+    _, low, _, high, _ = sides(nz)[0]
+    assert np.abs(low[:, :-step]).max() == 0 and np.abs(high[:, step:]).max() == 0
+
+    def kernel(u_hbm, c_hbm, u_ref, out_ref, up_ref, down_ref, c_ref, u_sem, c_sem):
         table_copy = pltpu.make_async_copy(c_hbm, c_ref, c_sem)
         copies = [
             pltpu.make_async_copy(
@@ -146,25 +157,33 @@
             )
             for i in range(steps)
         ]
+        for i in order[:flight]:
+            copies[i].start()
         table_copy.start()
-        for copy in copies:
-            copy.start()
         table_copy.wait()
         table = c_ref[...]
-        for i, copy in enumerate(copies):
-            copy.wait()
+        for turn, i in enumerate(order):
+            copies[i].wait()
+            if turn + flight < steps:
+                copies[order[turn + flight]].start()
             for p in range(i * step // 2, (i + 1) * step // 2):
                 parts = []
                 for z in (2 * p, 2 * p + 1):
                     hi, lo = split(u_ref[z])
                     parts += [hi, hi, lo]
                 out_ref[24 * p : 24 * p + 24, :] = dot(table, jnp.concatenate(parts, axis=0))
+            if i in order[:2]:
+                combos, ref = (high, down_ref) if i == 0 else (low, up_ref)
+                for c in range(2):
+                    ref[c * nx : c * nx + nx, :] = weighted(
+                        [(combos[c, z], lambda z=z: u_ref[z]) for z in range(i * step, (i + 1) * step)]
+                    )
 
     return pl.pallas_call(
         kernel,
         in_specs=[HB, HB],
-        out_specs=[VM, VM],
-        out_shape=[vmem((nz, nx, ny)), vmem((nz * 12, ny))],
+        out_specs=[VM] * 4,
+        out_shape=[vmem((nz, nx, ny)), vmem((nz * 12, ny)), vmem((2 * nx, ny)), vmem((2 * nx, ny))],
         scratch_shapes=[
             pltpu.VMEM(pair.shape, BF),
             pltpu.SemaphoreType.DMA((steps,)),
@@ -229,7 +248,7 @@
             at = 0
             for ref, eref, n in zip((x1, x2, x3), (e1, e2, e3), counts):
                 where = pl.ds(pl.multiple_of((i * step + z) * n, 16), n)
-                ref[where, :] = got[at : at + n]
+                ref[i * step + z] = got[at : at + n]
                 eref[where, :] = estack[at : at + n]
                 at += n
 
@@ -254,7 +273,7 @@
         grid=(steps,),
         in_specs=[VM] * 4,
         out_specs=[VM] * 5,
-        out_shape=[vmem((nz * n, ny)) for n in counts] + [jax.ShapeDtypeStruct((24, 512), F32)] * 2,
+        out_shape=[vmem((nz, n, ny)) for n in counts] + [jax.ShapeDtypeStruct((24, 512), F32)] * 2,
         scratch_shapes=[pltpu.VMEM((nz * n, 384), BF) for n in counts],
         compiler_params=params(24),
         name="x_apply",
@@ -278,38 +297,45 @@
     return total
 
 
-def z_combine(xs, nz):
-    ny = xs[0].shape[1]
+def z_combine(x2, x3, halo):
+    nz, _, ny = x2.shape
     tables = [t for t, _ in z_tables(nz)]
-    counts = [x.shape[0] // nz for x in xs]
-
-    def kernel(x1, x2, x3, o1, o2, o3):
-        for ref, out, table, n in zip((x1, x2, x3), (o1, o2, o3), tables, counts):
+    counts = [x2.shape[1], x3.shape[1]]
+    groups = ny // 128
+
+    def kernel(x2, x3, r_ref, o2, o3, of):
+        for ref, out, table, n in zip((x2, x3), (o2, o3), tables[1:], counts):
 
             def body(k, _, ref=ref, out=out, table=table, n=n):
-                row = pl.multiple_of((k // (ny // 128)) * 8, 8)
-                lane = pl.multiple_of((k % (ny // 128)) * 128, 128)
+                row = pl.multiple_of((k // groups) * 8, 8)
+                lane = pl.multiple_of((k % groups) * 128, 128)
                 get = {}
                 for z in range(nz):
                     if np.abs(table[:, z]).max() > 1e-12:
-                        get[z] = ref[pl.ds(pl.multiple_of(z * n + row, 8), 8), pl.ds(lane, 128)]
+                        get[z] = ref[z, pl.ds(row, 8), pl.ds(lane, 128)]
                 for c in range(table.shape[0]):
                     out[pl.ds(pl.multiple_of(c * n + row, 8), 8), pl.ds(lane, 128)] = weighted(
                         [(table[c, z], lambda z=z: get[z]) for z in range(nz)]
                     )
                 return 0
 
-            lax.fori_loop(0, (n // 8) * (ny // 128), body, 0)
+            lax.fori_loop(0, (n // 8) * groups, body, 0)
+        for c in range(4):
+            got = weighted(
+                [(tables[0][c, z], lambda z=z: r_ref[12 * z : 12 * z + 12, :]) for z in range(nz)]
+            )
+            of[4 * c : 4 * c + 2, :] = got[0:2]
+            of[4 * c + 2 : 4 * c + 4, :] = got[6:8]
 
     return pl.pallas_call(
         kernel,
         in_specs=[VM] * 3,
         out_specs=[VM] * 3,
-        out_shape=[vmem((t.shape[0] * n, ny)) for t, n in zip(tables, counts)],
+        out_shape=[vmem((t.shape[0] * n, ny)) for t, n in zip(tables[1:], counts)] + [vmem((16, ny))],
         compiler_params=params(16),
         cost_estimate=pl.CostEstimate(flops=20_000_000, bytes_accessed=6_000_000, transcendentals=0),
         name="z_combine",
-    )(*xs)
+    )(x2, x3, halo)
 
 
 def y_tables(ny, spread):
@@ -329,34 +355,79 @@
     return start + chunk * LEFT_RANKS[level]
 
 
-def halo_table(left, right, level, chunks, nz, counts):
-    base = np.zeros((48, left.shape[1]))
-    for chunk in chunks:
+LEFT_AT, RIGHT_AT = 32, 56
+
+
+def halo_base(left, right, level, nz, counts):
+    base = np.zeros((128, left.shape[1]))
+    for chunk in range(nz * counts[level] // 512):
         row = halo_rows(level, chunk, nz, counts)
-        base[row : row + left.shape[0]] = left
-        base[24 + row : 24 + row + right.shape[0]] = right
-    hi, lo = hi_lo(base)
-    none = np.zeros((32, left.shape[1]), hi.dtype)
-    return np.concatenate([hi, hi, none, lo, np.zeros_like(hi), none])
+        base[LEFT_AT + row : LEFT_AT + row + left.shape[0]] = left
+        base[RIGHT_AT + row : RIGHT_AT + row + right.shape[0]] = right
+    return base
 
 
 def turned(left_ref, right_ref):
-    both = jnp.concatenate([left_ref[...], right_ref[...]], axis=0)
-    hi = both.astype(BF).astype(F32)
-    wide = jnp.concatenate([hi, both - hi, jnp.zeros((32, 512), F32)], axis=0)
+    wide = jnp.concatenate(
+        [jnp.zeros((LEFT_AT, 512), F32), left_ref[...], right_ref[...], jnp.zeros((48, 512), F32)], axis=0
+    )
     return wide.T
 
 
-def y_messages(combined, from_left, from_right, nz):
-    ny = combined[0].shape[1]
+def band_tables(level, nz, counts, ny):
+    assert ny == 512
+    main, left, right = y_tables(ny, True)[level]
+    base = halo_base(left, right, level, nz, counts)
+    own, edge = [], []
+    for j in range(2):
+        cols = slice(256 * j, 256 * j + 256)
+        own.append(stack_rhs(main[cols, cols]))
+        tile = base[:, cols].copy()
+        if j == 0:
+            tile[:32] = main[256:288, cols]
+            assert np.abs(main[288:, cols]).max() == 0
+        else:
+            tile[96:] = main[224:256, cols]
+            assert np.abs(main[:224, cols]).max() == 0
+        edge.append(stack_rhs(tile))
+    return np.stack(own), np.stack(edge)
+
+
+def three(values):
+    hi, lo = split(values)
+    return jnp.concatenate([hi, lo, hi], axis=1)
+
+
+def banded(rows, edge, own_ref, edge_ref):
+    edges = three(edge)
+    out = []
+    for j in range(2):
+        own = three(rows[:, 256 * j : 256 * j + 256])
+        out.append(dot(own, own_ref[j]) + dot(edges, edge_ref[j]))
+    return jnp.concatenate(out, axis=1)
+
+
+def plain_edge(rows):
+    lanes = lax.broadcasted_iota(jnp.int32, (rows.shape[0], 128), 1)
+    before = jnp.where(lanes >= 96, rows[:, 128:256], 0.0)
+    return jnp.where(lanes < 32, rows[:, 256:384], before)
+
+
+def late_rows(counts, ny):
+    return [3 * counts[1] * (ny // 2) // ny, 4 * counts[2] * (ny // 4) // ny, 8, 8]
+
+
+def y_messages(combined, from_left, from_right, nz, band_one):
+    c2, c3, cf = combined
+    ny = c2.shape[1]
     tables = z_tables(nz)
     nums = [t.shape[0] for t, _ in tables]
-    counts = [c.shape[0] // n for c, n in zip(combined, nums)]
+    counts = [2 * c2.shape[0] // nums[1], c2.shape[0] // nums[1], c3.shape[0] // nums[2]]
     mains, halos, coefs = [], [], []
     for level, (main, left, right) in enumerate(y_tables(ny, False)):
         mains.append(stack_rhs(main))
+        halos.append(stack_rhs(halo_base(left, right, level, nz, counts)))
         chunks = nz * counts[level] // 512
-        halos.append(halo_table(left, right, level, range(chunks), nz, counts))
         per = 512 // counts[level]
         table = tables[level][0]
         coef = np.zeros((nums[level], per, 128), np.float32)
@@ -365,71 +436,81 @@
                 for chunk in range(chunks):
                     row = halo_rows(level, chunk, nz, counts)
                     for lane in range(LEFT_RANKS[level]):
-                        for base in (0, 24, 48, 72):
+                        for base in (LEFT_AT, RIGHT_AT):
                             coef[c, zz, base + row + lane] = table[c, chunk * per + zz]
         coefs.append(coef.reshape(nums[level] * per, 128))
-    heights = [(nums[0] // 2) * counts[0], 3 * counts[1] // 2, 4 * counts[2] // 4]
+    heights = late_rows(counts, ny)
     height = sum(heights)
-    height += -height % 8
-
-    def kernel(c1, c2, c3, fl, fr, m1, m2, m3, h1, h2, h3, k1, k2, k3, right_ref, left_ref):
+
+    def kernel(c2, c3, cf, fl, fr, own1, edge1, m2, m3, h2, h3, k1, k2, k3, up_ref, down_ref):
         halo = turned(fl, fr)
-        got = []
-        for c_ref, m, h, k, n, num in zip(
-            (c1, c2, c3), (m1, m2, m3), (h1, h2, h3), (k1, k2, k3), counts, nums
-        ):
+
+        def reduced(k, n, num):
             per = 512 // n
             extra = []
             for c in range(num):
                 total = None
                 for zz in range(per):
-                    term = halo[zz * n : zz * n + n] * k[c * per + zz : c * per + zz + 1, :]
-                    total = term if total is None else total + term
+                    if np.abs(coefs_of[n][c * per + zz]).max() > 1e-12:
+                        term = halo[zz * n : zz * n + n] * k[c * per + zz : c * per + zz + 1, :]
+                        total = term if total is None else total + term
                 extra.append(total)
-            ehi, elo = split(jnp.concatenate(extra, axis=0))
-            hi, lo = split(c_ref[...])
-            got.append(
-                dot(jnp.concatenate([hi, lo, hi], axis=1), m[...])
-                + dot(jnp.concatenate([ehi, ehi], axis=1), h[...])
-                + dot(elo, h[:128])
-            )
-        for side, ref in enumerate((right_ref, left_ref)):
+            return extra
+
+        coefs_of = dict(zip(counts, coefs))
+        got = []
+        for c_ref, m, h, k, n, num in zip((c2, c3), (m2, m3), (h2, h3), (k2, k3), counts[1:], nums[1:]):
+            extra = jnp.concatenate(reduced(k, n, num), axis=0)
+            got.append(dot(three(c_ref[...]), m[...]) + dot(three(extra), h[...]))
+        frame = cf[...]
+        frame = banded(frame, plain_edge(frame), own1, edge1)
+        ones = reduced(k1, counts[0], 4)
+        rows8 = lax.broadcasted_iota(jnp.int32, (8, 128), 0)
+        for side, ref in enumerate((up_ref, down_ref)):
             at = 0
-            for level in range(3):
+            for level in (1, 2):
                 n, width = counts[level], ny >> level
                 ranks = LEFT_RANKS if side == 0 else RIGHT_RANKS
                 first = 0 if side == 0 else LEFT_RANKS[level] * n
                 total = ranks[level] * n
-                per_row = ny // width
-                tall = heights[level]
-                for part in range(per_row):
-                    use = min(tall, total - part * tall)
+                tall = heights[level - 1]
+                for part in range(1 << level):
+                    use = max(min(tall, total - part * tall), 0)
+                    lanes = slice(part * width, (part + 1) * width)
                     if use > 0:
-                        ref[at : at + use, part * width : (part + 1) * width] = got[level][
+                        ref[at : at + use, lanes] = got[level - 1][
                             first + part * tall : first + part * tall + use
                         ]
                     if use < tall:
-                        use = max(use, 0)
-                        ref[at + use : at + tall, part * width : (part + 1) * width] = jnp.zeros(
-                            (tall - use, width), F32
-                        )
+                        ref[at + use : at + tall, lanes] = jnp.zeros((tall - use, width), F32)
                 at += tall
-            if at < height:
-                ref[at:, :] = jnp.zeros((height - at, ny), F32)
+            ref[at : at + 8, :] = frame[8 * side : 8 * side + 8]
+            at += 8
+            turn = jnp.concatenate(ones[2 * side : 2 * side + 2], axis=0).T
+            both = []
+            for start in (LEFT_AT, RIGHT_AT):
+                v = turn[start : start + 8]
+                v = v + pltpu.roll(v, 4, 0)
+                both.append(v + pltpu.roll(v, 2, 0))
+            ref[at:, :128] = jnp.where(rows8 < 2, both[0], both[1])
+            ref[at:, 128:] = jnp.zeros((8, ny - 128), F32)
 
     return pl.pallas_call(
         kernel,
         in_specs=[VM] * 14,
         out_specs=[VM] * 2,
-        out_shape=[jax.ShapeDtypeStruct((height, ny), F32)] * 2,
+        out_shape=[vmem((height, ny))] * 2,
         compiler_params=params(24),
         name="y_messages",
     )(
-        *combined,
+        c2,
+        c3,
+        cf,
         from_left,
         from_right,
-        *[jnp.asarray(t) for t in mains],
-        *[jnp.asarray(t) for t in halos],
+        *band_one,
+        *[jnp.asarray(t) for t in mains[1:]],
+        *[jnp.asarray(t) for t in halos[1:]],
         *[jnp.asarray(t) for t in coefs],
     )
 
@@ -469,120 +550,152 @@
     return [z for z in range(nz) if hit(z)]
 
 
-def main_part(xs, from_left, from_right, nz):
-    ny = xs[0].shape[1]
-    untouched = [z for z in range(nz) if z not in touched_layers(nz)]
-    counts = [x.shape[0] // nz for x in xs]
-    mains, halos = [], []
-    for level, (main, left, right) in enumerate(y_tables(ny, True)):
-        mains.append(stack_rhs(main))
+def main_part(xs, from_left, from_right, below, above, bands):
+    nz, nx, ny = xs[0].shape
+    counts = [nx, nx // 2, nx // 4]
+    changed = touched_layers(nz)
+    untouched = [z for z in range(nz) if z not in changed]
+    groups = ny // 128
+    _, _, maps = joint_sides(nx)
+    x_table = stack_lhs(maps[0][0])
+    masks = []
+    for level in range(3):
         chunks = nz * counts[level] // 512
-        halos.append(
-            np.stack([halo_table(left, right, level, [c], nz, counts) for c in range(chunks)])
-        )
-
-    def kernel(x1, x2, x3, fl, fr, m1, m2, m3, h1, h2, h3, out_ref, hbm, y1, y2, y3, w2, halo_ref, sem):
-        halo = turned(fl, fr).astype(BF)
-        halo_ref[...] = jnp.concatenate([halo, halo], axis=1)
-        for x, m, h, y, n in zip((x1, x2, x3), (m1, m2, m3), (h1, h2, h3), (y1, y2, y3), counts):
-
-            def chunk_body(j, _, x=x, m=m, h=h, y=y):
-                where = pl.ds(pl.multiple_of(j * 512, 512), 512)
-                hi, lo = split(x[where, :])
-                y[where, :] = dot(jnp.concatenate([hi, lo, hi], axis=1), m[...]) + dot(
-                    halo_ref[...], h[j]
+        mask = np.zeros((chunks, 128), np.float32)
+        for chunk in range(chunks):
+            row = halo_rows(level, chunk, nz, counts)
+            for base in (LEFT_AT, RIGHT_AT):
+                mask[chunk, base + row : base + row + LEFT_RANKS[level]] = 1.0
+        masks.append(mask)
+    mask_rows = np.concatenate(masks + [np.zeros((8 - sum(m.shape[0] for m in masks) % 8, 128), np.float32)])
+    mask_at = [0, masks[0].shape[0], masks[0].shape[0] + masks[1].shape[0]]
+
+    def kernel(x1, x2, x3, fl, fr, b1, a1, o1, e1, o2, e2, o3, e3, xt, mk, out_ref, w_ref, hbm, w2, halo_ref, sem):
+        halo_ref[...] = turned(fl, fr)
+        lanes = lax.broadcasted_iota(jnp.int32, (8, 128), 1)
+        after, before = lanes < 32, lanes >= 96
+
+        def in_y(x, level, row, own, edge):
+            n = counts[level]
+            per = 512 // n
+            values = x[:, pl.ds(row, 8), :]
+            edges = []
+            for z in range(nz):
+                at = mask_at[level] + z // per
+                turn = halo_ref[pl.ds(pl.multiple_of((z % per) * n + row, 8), 8), :] * mk[at : at + 1, :]
+                edges.append(
+                    jnp.where(after, values[z, :, 256:384], jnp.where(before, values[z, :, 128:256], turn))
                 )
-                return 0
-
-            lax.fori_loop(0, nz * n // 512, chunk_body, 0)
-
-        groups = ny // 128
-
-        def place(k):
-            return pl.multiple_of((k // groups) * 8, 8), pl.multiple_of((k % groups) * 128, 128)
-
-        def loaded(ref, n, row, lane):
-            return {
-                z: ref[pl.ds(pl.multiple_of(z * n + row, 8), 8), pl.ds(lane, 128)] for z in range(nz)
-            }
+            got = banded(
+                values.reshape(nz * 8, ny), jnp.concatenate(edges, axis=0), own, edge
+            )
+            return {z: got[8 * z : 8 * z + 8] for z in range(nz)}
+
+        def store(to, values, row, indices, height=None):
+            for z in indices:
+                for q in range(groups):
+                    piece = values[z][:, 128 * q : 128 * q + 128]
+                    if height is None:
+                        to[q, z, pl.ds(row, 8), :] = piece
+                    else:
+                        to[q, pl.ds(pl.multiple_of(z * height + row, 8), 8), :] = piece
 
         def level_one(k, _):
-            row, lane = place(k)
-            got = open_lift(loaded(y1, counts[0], row, lane), 0, nz - 1)
-            for z in range(nz):
-                out_ref[k % groups, z, pl.ds(row, 8), :] = got[z]
+            row = pl.multiple_of(k * 8, 8)
+            got = open_lift(in_y(x1, 0, row, o1, e1), 0, nz - 1)
+            store(out_ref, got, row, range(nz))
             return 0
 
-        lax.fori_loop(0, (counts[0] // 8) * groups, level_one, 0)
+        lax.fori_loop(0, counts[0] // 8, level_one, 0)
+
+        def leaving(layers):
+            return [
+                pltpu.make_async_copy(
+                    out_ref.at[q, z], hbm.at[z, :, 128 * q : 128 * q + 128], sem.at[z]
+                )
+                for z in layers
+                for q in range(groups)
+            ]
+
+        copies = leaving([z for z in untouched if z % 2])
+        for copy in copies:
+            copy.start()
 
         def lows(values, first, last):
             got = open_lift(values, 2 * first, 2 * last)
             return {i: got[2 * i] for i in range(first, last + 1) if got[2 * i] is not None}
 
         def level_two(k, _):
-            row, lane = place(k)
-            one = lows(loaded(y2, counts[1], row, lane), -2, nz // 2 + 1)
-            got = open_lift(one, 0, nz // 2 - 1)
-            for z in range(nz // 2):
-                w2[k % groups, pl.ds(pl.multiple_of(z * counts[1] + row, 8), 8), :] = got[z]
+            row = pl.multiple_of(k * 8, 8)
+            one = lows(in_y(x2, 1, row, o2, e2), -2, nz // 2 + 1)
+            store(w2, open_lift(one, 0, nz // 2 - 1), row, range(nz // 2), counts[1])
             return 0
 
-        lax.fori_loop(0, (counts[1] // 8) * groups, level_two, 0)
-
-        lane_ids = lax.broadcasted_iota(jnp.int32, (8, 128), 1)
+        lax.fori_loop(0, counts[1] // 8, level_two, 0)
 
         def level_three(k, _):
-            row, lane = place(k)
-            one = lows(loaded(y3, counts[2], row, lane), -2, nz // 2 + 1)
+            row = pl.multiple_of(k * 8, 8)
+            one = lows(in_y(x3, 2, row, o3, e3), -2, nz // 2 + 1)
             two = lows(one, -3, nz // 4 + 2)
             got = open_lift(two, 0, nz // 4 - 1)
             for z in range(nz // 4):
                 where = pl.ds(2 * z * counts[1] + 2 * row, 8, stride=2)
-                old = w2[k % groups, where, :]
-                w2[k % groups, where, :] = jnp.where(lane_ids % 4 == 0, got[z], old)
+                for q in range(groups):
+                    piece = got[z][:, 128 * q : 128 * q + 128]
+                    w2[q, where, :] = jnp.where(lanes % 4 == 0, piece, w2[q, where, :])
             return 0
 
-        lax.fori_loop(0, (counts[2] // 8) * groups, level_three, 0)
+        lax.fori_loop(0, counts[2] // 8, level_three, 0)
 
         def merge(k, _):
-            row, _ = place(k)
+            row = pl.multiple_of((k // groups) * 8, 8)
+            q = k % groups
+            where = pl.ds(2 * row, 8, stride=2)
             for z in range(nz // 2):
-                inner = w2[k % groups, pl.ds(pl.multiple_of(z * counts[1] + row, 8), 8), :]
-                where = pl.ds(2 * row, 8, stride=2)
-                old = out_ref[k % groups, 2 * z, where, :]
-                out_ref[k % groups, 2 * z, where, :] = jnp.where(lane_ids % 2 == 0, inner, old)
+                inner = w2[q, pl.ds(pl.multiple_of(z * counts[1] + row, 8), 8), :]
+                out_ref[q, 2 * z, where, :] = jnp.where(lanes % 2 == 0, inner, out_ref[q, 2 * z, where, :])
             return 0
 
         lax.fori_loop(0, (counts[1] // 8) * groups, merge, 0)
-
-        copies = [
-            pltpu.make_async_copy(
-                out_ref.at[q, z], hbm.at[z, :, 128 * q : 128 * q + 128], sem.at[z]
-            )
-            for z in untouched
-            for q in range(groups)
-        ]
-        for copy in copies:
+        more = leaving([z for z in untouched if z % 2 == 0])
+        for copy in more:
             copy.start()
-        for copy in copies:
+
+        early = []
+        for ref in (b1, a1):
+            for c in range(2):
+                hi, lo = split(ref[c * nx : c * nx + nx, :])
+                early.append(dot(xt[...], jnp.concatenate([hi, hi, lo], axis=0)))
+        early = jnp.concatenate(early, axis=0)
+        w_ref[...] = banded(early, plain_edge(early), o1, e1)
+
+        for copy in copies + more:
             copy.wait()
 
+    flat = [t for band in bands for t in band]
     return pl.pallas_call(
         kernel,
-        in_specs=[VM] * 11,
-        out_specs=[VM, HB],
-        out_shape=[vmem((ny // 128, nz, counts[0], 128)), pltpu.HBM((nz, counts[0], ny), F32)],
-        scratch_shapes=[pltpu.VMEM((nz * n, ny), F32) for n in counts]
-        + [pltpu.VMEM((ny // 128, nz // 2 * counts[1], 128), F32), pltpu.VMEM((512, 256), BF), pltpu.SemaphoreType.DMA((nz,))],
+        in_specs=[VM] * 15,
+        out_specs=[VM, VM, HB],
+        out_shape=[
+            vmem((groups, nz, nx, 128)),
+            vmem((4 * nx, ny)),
+            pltpu.HBM((nz, nx, ny), F32),
+        ],
+        scratch_shapes=[
+            pltpu.VMEM((groups, nz // 2 * counts[1], 128), F32),
+            pltpu.VMEM((512, 128), F32),
+            pltpu.SemaphoreType.DMA((nz,)),
+        ],
         compiler_params=params(32),
         cost_estimate=pl.CostEstimate(
             flops=8_000_000_000, bytes_accessed=20_000_000, transcendentals=0
         ),
         name="main_part",
-    )(*xs, from_left, from_right, *[jnp.asarray(t) for t in mains], *[jnp.asarray(t) for t in halos])
-
-
-def z_apply(inner, partial, from_left, from_right):
+    )(*xs, from_left, from_right, below, above, *flat, jnp.asarray(x_table), jnp.asarray(mask_rows))
+
+
+def z_apply(inner, partial, early, from_left, from_right):
     groups, nz, nx, _ = inner.shape
     ny = groups * 128
     maps = [p for _, p in z_tables(nz)]
@@ -592,20 +705,39 @@
         width = ny >> level
         hi = spread_columns(np.eye(width), 1 << level, ny).astype(ml_dtypes.bfloat16)
         tables.append(np.concatenate([hi, hi]))
-    heights = [2 * counts[0], 3 * counts[1] // 2, 4 * counts[2] // 4]
+    heights = late_rows(counts, ny)
+    _, _, x_maps = joint_sides(nx)
+    frame = np.zeros((4 * nx, 16))
+    for c in range(4):
+        frame[c * nx : c * nx + nx, 4 * c : 4 * c + 2] = x_maps[0][1][:, :2]
+        frame[c * nx : c * nx + nx, 4 * c + 2 : 4 * c + 4] = x_maps[0][2][:, :2]
+        assert np.abs(x_maps[0][1][:, 2:]).max() < 1e-12 and np.abs(x_maps[0][2][:, 2:]).max() < 1e-12
+    _, left, right = y_tables(ny, True)[0]
+    side_rows = np.zeros((128, ny))
+    side_rows[:2], side_rows[2:4] = left, right
     touched = touched_layers(nz)
 
-    def kernel(in_ref, base_hbm, fl, fr, t2, t3, out_hbm, s1, s2, s3, buf, sem):
+    def kernel(in_ref, base_hbm, w_ref, fl, fr, t2, t3, xf, yf, out_hbm, s1, s2, s3, buf, sem):
         del base_hbm
         s3[...] = jnp.zeros(s3.shape, F32)
+        at = heights[0] + heights[1]
+        hi, lo = split(jnp.concatenate([fl[at : at + 8, :], fr[at : at + 8, :]], axis=0))
+        at += 8
+        none = jnp.zeros((120, 128), F32)
+        turn = [jnp.concatenate([ref[at : at + 8, :128], none], axis=0).T for ref in (fl, fr)]
+        first = (
+            w_ref[...]
+            + dot(xf[...], jnp.concatenate([hi, hi, lo], axis=0))
+            + dot(three(jnp.concatenate(turn, axis=0)), yf[...])
+        )
+        for c in range(4):
+            for q in range(groups):
+                s1[c, q] = first[c * nx : c * nx + nx, 128 * q : 128 * q + 128]
         for side, ref in enumerate((fl, fr)):
-            for c in range(2):
-                for q in range(groups):
-                    s1[2 * side + c, q] = ref[c * nx : c * nx + nx, 128 * q : 128 * q + 128]
             ranks = LEFT_RANKS if side == 0 else RIGHT_RANKS
-            at = heights[0]
+            at = 0
             for level, table, to in ((1, t2, s2), (2, t3, s3)):
-                width, tall, n = ny >> level, heights[level], counts[level]
+                width, tall, n = ny >> level, heights[level - 1], counts[level]
                 flat = jnp.concatenate(
                     [ref[at : at + tall, p * width : p * width + width] for p in range(1 << level)],
                     axis=0,
@@ -674,7 +806,7 @@
 
     return pl.pallas_call(
         kernel,
-        in_specs=[VM, HB, VM, VM, VM, VM],
+        in_specs=[VM, HB] + [VM] * 7,
         out_specs=HB,
         out_shape=jax.ShapeDtypeStruct((nz, nx, ny), F32),
         input_output_aliases={1: 0},
@@ -687,7 +819,16 @@
         ],
         compiler_params=params(24),
         name="z_apply",
-    )(inner, partial, from_left, from_right, *[jnp.asarray(t) for t in tables])
+    )(
+        inner,
+        partial,
+        early,
+        from_left,
+        from_right,
+        *[jnp.asarray(t) for t in tables],
+        jnp.asarray(stack_lhs(frame)),
+        jnp.asarray(stack_rhs(side_rows)),
+    )
 
 
 def swap(to_right, to_left, axis):
@@ -698,16 +839,19 @@
 
 
 def local(field):
-    nz = field.shape[0]
-    field, message = x_send(field)
+    nz, nx, ny = field.shape
+    counts = [nx, nx // 2, nx // 4]
+    bands = [[jnp.asarray(t) for t in band_tables(level, nz, counts, ny)] for level in range(3)]
+    field, message, up, down = x_send(field)
     halo = x_exchange(message)
+    below, above = swap(up, down, "gz")
     x1, x2, x3, to_right, to_left = x_apply(field, halo)
     from_left, from_right = swap(to_right, to_left, "gy")
-    combined = z_combine((x1, x2, x3), nz)
-    to_right, to_left = y_messages(combined, from_left, from_right, nz)
-    below, above = swap(to_right, to_left, "gz")
-    inner, partial = main_part((x1, x2, x3), from_left, from_right, nz)
-    return z_apply(inner, partial, below, above)
+    combined = z_combine(x2, x3, halo)
+    up, down = y_messages(combined, from_left, from_right, nz, bands[0])
+    late_below, late_above = swap(up, down, "gz")
+    inner, early, partial = main_part((x1, x2, x3), from_left, from_right, below, above, bands)
+    return z_apply(inner, partial, early, late_below, late_above)
 
 
 def solution(mesh):

time: 40.3 us -> 36.7 us (0.911)
  Pallas kernels: 26.8 us -> 22.2 us
  starting transfers between devices: 8.32 us -> 12.1 us
  waiting for transfers between devices: 4.77 us -> 1.72 us
    ppermute x2 -> x3, starting transfers between devices: 3.27 us -> 7.1 us  [swap(): lax.ppermute(to_left, axis, left)]
    pallas_call x3, Pallas kernels: 20.9 us -> 17.6 us  [the longest x1 10.8 us: main_part(): pl.pallas_call(kernel, in_specs=[VM] * 15, out_specs=[VM, VM, HB], out_sh...]
    ppermute x2 -> x3, waiting for transfers between devices: 2.85 us -> 0.52 us  [swap(): lax.ppermute(to_left, axis, left)]
    ppermute x1, waiting for transfers between devices: 1.91 us -> 0.01 us  [x_exchange(): return lax.ppermute(message, 'gx', right)]
    ppermute x2 -> x3, waiting for transfers between devices: 0.01 us -> 1.2 us  [swap(): lax.ppermute(to_right, axis, right)]
    pallas_call x1, Pallas kernels: 2.15 us -> 1.09 us  [z_combine(): pl.pallas_call(kernel, in_specs=[VM] * 3, out_specs=[VM] * 3, out_shape=[...]
    ppermute x2 -> x3, starting transfers between devices: 4.54 us -> 4.5 us  [swap(): lax.ppermute(to_right, axis, right)]
  transfers between devices with their start and end apart: 5 -> 7, of which waited for: 3 -> 2; matrix products, arithmetic and copies ran while one was open for 0% -> 0% of each run, Pallas kernels for 41% -> 42%
where the time goes in v2:
time: 36.7 us; the launch traced here: 36.5 us
  Pallas kernels  22.2 us (60%)
  starting transfers between devices  12.1 us (33%)
  waiting for transfers between devices  1.72 us (5%)
    pallas_call x1, Pallas kernels, main_part(): pl.pallas_call(kernel, in_specs=[VM] * 15, out_specs=[VM, VM, HB], out_sh...  10.8 us
    ppermute x3, starting transfers between devices, swap(): lax.ppermute(to_left, axis, left)  7.1 us
    ppermute x3, starting transfers between devices, swap(): lax.ppermute(to_right, axis, right)  4.5 us
    pallas_call x1, Pallas kernels, x_send(): pl.pallas_call(kernel, in_specs=[HB, HB], out_specs=[VM] * 4, out_shape=[...  4.08 us
    pallas_call x1, Pallas kernels, z_apply(): pl.pallas_call(kernel, in_specs=[VM, HB] + [VM] * 7, out_specs=HB, out_sh...  2.75 us
    pallas_call x1, Pallas kernels, x_apply(): pl.pallas_call(kernel, grid=(steps,), in_specs=[VM] * 4, out_specs=[VM] *...  2.64 us
    ppermute x3, waiting for transfers between devices, swap(): lax.ppermute(to_right, axis, right)  1.2 us
    pallas_call x1, Pallas kernels, z_combine(): pl.pallas_call(kernel, in_specs=[VM] * 3, out_specs=[VM] * 3, out_shape=[...  1.09 us
  transfers between devices with their start and end apart: 7, of which 2 were waited for; matrix products, arithmetic and copies ran while one was open for 0% of the time, Pallas kernels for 42%

profile of v2, /device:TPU:0, one launch (start us, length us, event | category | flops | bytes accessed | tf_op | source)
XLA Modules:
  0.0 36.5 jit_solution(11953309971305937422)
XLA Ops:
  0.0 4.1 %x_send.1 = (f32[32,64,512]{2,1,0:T(8,128)S(1)}, f32[384,512]{1,0:T(8,128)S(1)}, f32[128,512]{1,0:T(8,128)S(1)}, f32[128,512]{1,0:T(8,128)S(1)}) custom-call(f32[32,64,512]{2,1,0:T(8,128)} %u_hbm.1, bf16[24,384]{1,0:T(8,128)(2,1)} %constant.50.clone.c_hbm), custom_call_target="tpu_custom_call" | custom-call | tf_op jit(solution)/shard_map/x_send/pallas_call | solution.py:182
  4.1 0.5 %collective-permute-start = (f32[384,512]{1,0:T(8,128)S(1)}, f32[384,512]{1,0:T(8,128)S(1)}, u32[]{:S(2)}, u32[]{:S(2)}) collective-permute-start(f32[384,512]{1,0:T(8,128)S(1)} %get-tuple-element.23), channel_id=1, source_target_pairs={{0,16},{16,0},{1,17},{17,1},{2,18},{18,2},{3,19},{19,3},{4,20},{20... | collective-permute-start | bytes 2359304 | tf_op jit(solution)/shard_map/ppermute | solution.py:201
  4.6 2.6 %collective-permute-start.3 = (f32[128,512]{1,0:T(8,128)S(1)}, f32[128,512]{1,0:T(8,128)S(1)}, u32[]{:S(2)}, u32[]{:S(2)}) collective-permute-start(f32[128,512]{1,0:T(8,128)S(1)} %get-tuple-element.29), channel_id=1, source_target_pairs={{0,1},{1,2},{2,3},{3,0},{4,5},{5,6},{6,7},{7,4},{8,9},{9,10},{10,1... | collective-permute-start | bytes 786440 | tf_op jit(solution)/shard_map/ppermute | solution.py:838
  7.3 2.1 %collective-permute-start.4 = (f32[128,512]{1,0:T(8,128)S(1)}, f32[128,512]{1,0:T(8,128)S(1)}, u32[]{:S(2)}, u32[]{:S(2)}) collective-permute-start(f32[128,512]{1,0:T(8,128)S(1)} %get-tuple-element.30), channel_id=1, source_target_pairs={{1,0},{2,1},{3,2},{0,3},{5,4},{6,5},{7,6},{4,7},{9,8},{10,9},{11,1... | collective-permute-start | bytes 786440 | tf_op jit(solution)/shard_map/ppermute | solution.py:838
  9.4 0.0 collective-permute-done.r_ref
  9.4 0.0 copy-done.13
  9.4 0.0 copy-done.9
  9.4 0.0 copy-start
  9.4 0.0 copy-start.1
  9.4 0.0 copy-start.3
  9.4 0.0 copy-start.4
  9.4 0.0 copy-start.7
  9.4 0.0 copy-start.8
  9.5 0.0 copy-start.10
  9.5 0.0 copy-start.12
  9.5 0.0 copy-start.14
  9.5 2.6 %x_apply.1 = (f32[32,64,512]{2,1,0:T(8,128)S(1)}, f32[32,32,512]{2,1,0:T(8,128)S(1)}, f32[32,16,512]{2,1,0:T(8,128)S(1)}, f32[24,512]{1,0:T(8,128)S(1)}, f32[24,512]{1,0:T(8,128)S(1)}) custom-call(f32[32,64,512]{2,1,0:T(8,128)S(1)} %get-tuple-element.22.u_ref, f32[384,512]{1,0:T(8,128)S(1)} %collective-permute-done.r_ref, ...), custom_call_target="tpu_custom_call" | custom-call | tf_op jit(solution)/shard_map/x_apply/pallas_call | solution.py:271
  12.1 0.0 copy-start.16
  12.2 0.0 copy-start.17
  12.2 0.0 copy-start.18
  12.2 0.0 copy-start.19
  12.2 0.0 copy-start.20
  12.2 1.7 %collective-permute-start.1 = (f32[24,512]{1,0:T(8,128)S(1)}, f32[24,512]{1,0:T(8,128)S(1)}, u32[]{:S(2)}, u32[]{:S(2)}) collective-permute-start(f32[24,512]{1,0:T(8,128)S(1)} %get-tuple-element.27), channel_id=1, source_target_pairs={{0,4},{4,8},{8,12},{12,0},{1,5},{5,9},{9,13},{13,1},{2,6},{6,10},{... | collective-permute-start | bytes 147464 | tf_op jit(solution)/shard_map/ppermute | solution.py:838
  13.9 1.3 %collective-permute-start.2 = (f32[24,512]{1,0:T(8,128)S(1)}, f32[24,512]{1,0:T(8,128)S(1)}, u32[]{:S(2)}, u32[]{:S(2)}) collective-permute-start(f32[24,512]{1,0:T(8,128)S(1)} %get-tuple-element.28), channel_id=1, source_target_pairs={{4,0},{8,4},{12,8},{0,12},{5,1},{9,5},{13,9},{1,13},{6,2},{10,6},{... | collective-permute-start | bytes 147464 | tf_op jit(solution)/shard_map/ppermute | solution.py:838
  15.2 1.1 %z_combine.1 = (f32[192,512]{1,0:T(8,128)S(1)}, f32[112,512]{1,0:T(8,128)S(1)}, f32[16,512]{1,0:T(8,128)S(1)}) custom-call(f32[32,32,512]{2,1,0:T(8,128)S(1)} %get-tuple-element.25.x2, f32[32,16,512]{2,1,0:T(8,128)S(1)} %get-tuple-element.26.x3, f32[384,512]{1,0:T(8,128)S(1)} %collective-permute-done.r_ref), custom_call_target="tpu_custom_call" | custom-call | flops 20000000 | bytes 6000000 | tf_op jit(solution)/shard_map/z_combine/pallas_call | solution.py:330
  16.3 1.2 %collective-permute-done.1.fl = f32[24,512]{1,0:T(8,128)S(1)} collective-permute-done((f32[24,512]{1,0:T(8,128)S(1)}, f32[24,512]{1,0:T(8,128)S(1)}, u32[]{:S(2)}, u32[]{:S(2)}) %collective-permute-start.1) | collective-permute-done | bytes 49184 | tf_op jit(solution)/shard_map/ppermute | solution.py:838
  17.5 0.5 %collective-permute-done.2.fr = f32[24,512]{1,0:T(8,128)S(1)} collective-permute-done((f32[24,512]{1,0:T(8,128)S(1)}, f32[24,512]{1,0:T(8,128)S(1)}, u32[]{:S(2)}, u32[]{:S(2)}) %collective-permute-start.2) | collective-permute-done | bytes 49184 | tf_op jit(solution)/shard_map/ppermute | solution.py:838
  18.0 0.0 copy-done
  18.0 0.0 copy-done.1
  18.0 0.0 copy-done.3
  18.1 0.9 %y_messages.1 = (f32[80,512]{1,0:T(8,128)S(1)}, f32[80,512]{1,0:T(8,128)S(1)}) custom-call(f32[192,512]{1,0:T(8,128)S(1)} %get-tuple-element.34.c2, f32[112,512]{1,0:T(8,128)S(1)} %get-tuple-element.35.c3, f32[16,512]{1,0:T(8,128)S(1)} %get-tuple-element.36.cf, f32[24,512]{1,0:T(8,128)S(1)} %collective-permute-done.1.fl, ...), custom_call_target="tpu_custom_call" | custom-call | tf_op jit(solution)/shard_map/y_messages/pallas_call | solution.py:498
  18.9 0.2 collective-permute-start.5
  19.1 3.7 %collective-permute-start.6 = (f32[80,512]{1,0:T(8,128)S(1)}, f32[80,512]{1,0:T(8,128)S(1)}, u32[]{:S(2)}, u32[]{:S(2)}) collective-permute-start(f32[80,512]{1,0:T(8,128)S(1)} %get-tuple-element.38), channel_id=1, source_target_pairs={{1,0},{2,1},{3,2},{0,3},{5,4},{6,5},{7,6},{4,7},{9,8},{10,9},{11,1... | collective-permute-start | bytes 491528 | tf_op jit(solution)/shard_map/ppermute | solution.py:838
  22.8 0.0 collective-permute-done.3.b1
  22.8 0.0 collective-permute-done.4.a1
  22.8 0.0 copy-done.15
  22.9 0.0 copy-start.2
  22.9 0.0 copy-start.5
  22.9 0.0 copy-start.6
  22.9 0.0 copy-start.11
  22.9 10.8 %main_part.1 = (f32[4,32,64,128]{3,2,1,0:T(8,128)S(1)}, f32[256,512]{1,0:T(8,128)S(1)}, f32[32,64,512]{2,1,0:T(8,128)}) custom-call(f32[32,64,512]{2,1,0:T(8,128)S(1)} %get-tuple-element.24.x1, f32[32,32,512]{2,1,0:T(8,128)S(1)} %get-tuple-element.25.x2, f32[32,16,512]{2,1,0:T(8,128)S(1)} %get-tuple-element.26.x3, f32[24,512]{1,0:T(8,128)S(1)} %collective-permute-done.1.fl, ...), custom_call_target="tpu_custom_call" | custom-call | flops 8000000000 | bytes 20000000 | tf_op jit(solution)/shard_map/main_part/pallas_call | solution.py:676
  33.7 0.0 collective-permute-done.5.fl
  33.8 0.0 collective-permute-done.6.fr
  33.8 0.0 copy-done.2
  33.8 0.0 copy-done.5
  33.8 0.0 copy-done.6
  33.8 0.0 copy-done.11
  33.8 2.7 %z_apply.1 = f32[32,64,512]{2,1,0:T(8,128)} custom-call(f32[4,32,64,128]{3,2,1,0:T(8,128)S(1)} %get-tuple-element.31.in_ref, f32[32,64,512]{2,1,0:T(8,128)} %get-tuple-element.32.base_hbm, f32[256,512]{1,0:T(8,128)S(1)} %get-tuple-element.33.w_ref, f32[80,512]{1,0:T(8,128)S(1)} %collective-permute-done.5.fl, ...), custom_call_target="tpu_custom_call", output_to_operand_aliasing={{}: (1, {})} | custom-call | tf_op jit(solution)/shard_map/z_apply/pallas_call | solution.py:807
  (14 shorter events, 0.0 us)
Async XLA Ops:
  0.0 9.4 %copy-start.13 = (bf16[3,8,384]{2,1,0:T(8,128)(2,1)S(1)}, bf16[3,8,384]{2,1,0:T(8,128)(2,1)}, u32[]{:S(2)}) copy-start(bf16[3,8,384]{2,1,0:T(8,128)(2,1)} %constant.52.clone.c_ref) | copy-start | bytes 55300
  0.0 9.4 %copy-start.9 = (bf16[2,112,240]{2,1,0:T(8,128)(2,1)S(1)}, bf16[2,112,240]{2,1,0:T(8,128)(2,1)}, u32[]{:S(2)}) copy-start(bf16[2,112,240]{2,1,0:T(8,128)(2,1)} %constant.51.clone.t_ref) | copy-start | bytes 322564
  4.1 5.3 %collective-permute-start = (f32[384,512]{1,0:T(8,128)S(1)}, f32[384,512]{1,0:T(8,128)S(1)}, u32[]{:S(2)}, u32[]{:S(2)}) collective-permute-start(f32[384,512]{1,0:T(8,128)S(1)} %get-tuple-element.23), channel_id=1, source_target_pairs={{0,16},{16,0},{1,17},{17,1},{2,18},{18,2},{3,19},{19,3},{4,20},{20... | collective-permute-start | bytes 2359304 | tf_op jit(solution)/shard_map/ppermute | solution.py:201
  4.6 18.2 %collective-permute-start.3 = (f32[128,512]{1,0:T(8,128)S(1)}, f32[128,512]{1,0:T(8,128)S(1)}, u32[]{:S(2)}, u32[]{:S(2)}) collective-permute-start(f32[128,512]{1,0:T(8,128)S(1)} %get-tuple-element.29), channel_id=1, source_target_pairs={{0,1},{1,2},{2,3},{3,0},{4,5},{5,6},{6,7},{7,4},{8,9},{9,10},{10,1... | collective-permute-start | bytes 786440 | tf_op jit(solution)/shard_map/ppermute | solution.py:838
  7.3 15.6 %collective-permute-start.4 = (f32[128,512]{1,0:T(8,128)S(1)}, f32[128,512]{1,0:T(8,128)S(1)}, u32[]{:S(2)}, u32[]{:S(2)}) collective-permute-start(f32[128,512]{1,0:T(8,128)S(1)} %get-tuple-element.30), channel_id=1, source_target_pairs={{1,0},{2,1},{3,2},{0,3},{5,4},{6,5},{7,6},{4,7},{9,8},{10,9},{11,1... | collective-permute-start | bytes 786440 | tf_op jit(solution)/shard_map/ppermute | solution.py:838
  9.4 8.6 %copy-start = (bf16[2,768,256]{2,1,0:T(8,128)(2,1)S(1)}, bf16[2,768,256]{2,1,0:T(8,128)(2,1)}, u32[]{:S(2)}) copy-start(bf16[2,768,256]{2,1,0:T(8,128)(2,1)} %constant.44.clone.o1.own1) | copy-start | bytes 2359300
  9.4 8.6 %copy-start.1 = (bf16[1536,256]{1,0:T(8,128)(2,1)S(1)}, bf16[1536,256]{1,0:T(8,128)(2,1)}, u32[]{:S(2)}) copy-start(bf16[1536,256]{1,0:T(8,128)(2,1)} %constant.53.clone.m2) | copy-start | bytes 2359300
  9.4 8.6 %copy-start.3 = (bf16[2,384,256]{2,1,0:T(8,128)(2,1)S(1)}, bf16[2,384,256]{2,1,0:T(8,128)(2,1)}, u32[]{:S(2)}) copy-start(bf16[2,384,256]{2,1,0:T(8,128)(2,1)} %constant.45.clone.e1.edge1) | copy-start | bytes 1179652
  9.4 8.6 %copy-start.4 = (bf16[1536,128]{1,0:T(8,128)(2,1)S(1)}, bf16[1536,128]{1,0:T(8,128)(2,1)}, u32[]{:S(2)}) copy-start(bf16[1536,128]{1,0:T(8,128)(2,1)} %constant.54.clone.m3) | copy-start | bytes 1179652
  9.4 8.6 %copy-start.7 = (bf16[384,256]{1,0:T(8,128)(2,1)S(1)}, bf16[384,256]{1,0:T(8,128)(2,1)}, u32[]{:S(2)}) copy-start(bf16[384,256]{1,0:T(8,128)(2,1)} %constant.55.clone.h2) | copy-start | bytes 589828
  9.4 8.6 %copy-start.8 = (f32[224,128]{1,0:T(8,128)S(1)}, f32[224,128]{1,0:T(8,128)}, u32[]{:S(2)}) copy-start(f32[224,128]{1,0:T(8,128)} %constant.59.clone.k3) | copy-start | bytes 344068
  9.5 8.6 %copy-start.10 = (bf16[384,128]{1,0:T(8,128)(2,1)S(1)}, bf16[384,128]{1,0:T(8,128)(2,1)}, u32[]{:S(2)}) copy-start(bf16[384,128]{1,0:T(8,128)(2,1)} %constant.56.clone.h3) | copy-start | bytes 294916
  9.5 8.6 %copy-start.12 = (f32[96,128]{1,0:T(8,128)S(1)}, f32[96,128]{1,0:T(8,128)}, u32[]{:S(2)}) copy-start(f32[96,128]{1,0:T(8,128)} %constant.58.clone.k2) | copy-start | bytes 147460
  9.5 8.6 %copy-start.14 = (f32[32,128]{1,0:T(8,128)S(1)}, f32[32,128]{1,0:T(8,128)}, u32[]{:S(2)}) copy-start(f32[32,128]{1,0:T(8,128)} %constant.57.clone.k1) | copy-start | bytes 49156
  12.1 10.7 %copy-start.15 = (bf16[2,768,256]{2,1,0:T(8,128)(2,1)S(1)}, bf16[2,768,256]{2,1,0:T(8,128)(2,1)}, u32[]{:S(2)}) copy-start(bf16[2,768,256]{2,1,0:T(8,128)(2,1)} %constant.48.clone.o3) | copy-start | bytes 2359300
  12.1 10.7 %copy-start.16 = (bf16[2,768,256]{2,1,0:T(8,128)(2,1)S(1)}, bf16[2,768,256]{2,1,0:T(8,128)(2,1)}, u32[]{:S(2)}) copy-start(bf16[2,768,256]{2,1,0:T(8,128)(2,1)} %constant.46.clone.o2) | copy-start | bytes 2359300
  12.2 10.7 %copy-start.17 = (bf16[2,384,256]{2,1,0:T(8,128)(2,1)S(1)}, bf16[2,384,256]{2,1,0:T(8,128)(2,1)}, u32[]{:S(2)}) copy-start(bf16[2,384,256]{2,1,0:T(8,128)(2,1)} %constant.49.clone.e3) | copy-start | bytes 1179652
  12.2 10.7 %copy-start.18 = (bf16[2,384,256]{2,1,0:T(8,128)(2,1)S(1)}, bf16[2,384,256]{2,1,0:T(8,128)(2,1)}, u32[]{:S(2)}) copy-start(bf16[2,384,256]{2,1,0:T(8,128)(2,1)} %constant.47.clone.e2) | copy-start | bytes 1179652
  12.2 10.7 %copy-start.19 = (bf16[64,192]{1,0:T(8,128)(2,1)S(1)}, bf16[64,192]{1,0:T(8,128)(2,1)}, u32[]{:S(2)}) copy-start(bf16[64,192]{1,0:T(8,128)(2,1)} %constant.60.clone.xt) | copy-start | bytes 73732
  12.2 10.7 %copy-start.20 = (f32[8,128]{1,0:T(8,128)S(1)}, f32[8,128]{1,0:T(8,128)}, u32[]{:S(2)}) copy-start(f32[8,128]{1,0:T(8,128)} %constant.61.clone.mk) | copy-start | bytes 12292
  12.2 5.3 %collective-permute-start.1 = (f32[24,512]{1,0:T(8,128)S(1)}, f32[24,512]{1,0:T(8,128)S(1)}, u32[]{:S(2)}, u32[]{:S(2)}) collective-permute-start(f32[24,512]{1,0:T(8,128)S(1)} %get-tuple-element.27), channel_id=1, source_target_pairs={{0,4},{4,8},{8,12},{12,0},{1,5},{5,9},{9,13},{13,1},{2,6},{6,10},{... | collective-permute-start | bytes 147464 | tf_op jit(solution)/shard_map/ppermute | solution.py:838
  13.9 4.1 %collective-permute-start.2 = (f32[24,512]{1,0:T(8,128)S(1)}, f32[24,512]{1,0:T(8,128)S(1)}, u32[]{:S(2)}, u32[]{:S(2)}) collective-permute-start(f32[24,512]{1,0:T(8,128)S(1)} %get-tuple-element.28), channel_id=1, source_target_pairs={{4,0},{8,4},{12,8},{0,12},{5,1},{9,5},{13,9},{1,13},{6,2},{10,6},{... | collective-permute-start | bytes 147464 | tf_op jit(solution)/shard_map/ppermute | solution.py:838
  18.9 14.8 %collective-permute-start.5 = (f32[80,512]{1,0:T(8,128)S(1)}, f32[80,512]{1,0:T(8,128)S(1)}, u32[]{:S(2)}, u32[]{:S(2)}) collective-permute-start(f32[80,512]{1,0:T(8,128)S(1)} %get-tuple-element.37), channel_id=1, source_target_pairs={{0,1},{1,2},{2,3},{3,0},{4,5},{5,6},{6,7},{7,4},{8,9},{9,10},{10,1... | collective-permute-start | bytes 491528 | tf_op jit(solution)/shard_map/ppermute | solution.py:838
  19.1 14.6 %collective-permute-start.6 = (f32[80,512]{1,0:T(8,128)S(1)}, f32[80,512]{1,0:T(8,128)S(1)}, u32[]{:S(2)}, u32[]{:S(2)}) collective-permute-start(f32[80,512]{1,0:T(8,128)S(1)} %get-tuple-element.38), channel_id=1, source_target_pairs={{1,0},{2,1},{3,2},{0,3},{5,4},{6,5},{7,6},{4,7},{9,8},{10,9},{11,1... | collective-permute-start | bytes 491528 | tf_op jit(solution)/shard_map/ppermute | solution.py:838
  22.9 10.9 %copy-start.2 = (bf16[512,512]{1,0:T(8,128)(2,1)S(1)}, bf16[512,512]{1,0:T(8,128)(2,1)}, u32[]{:S(2)}) copy-start(bf16[512,512]{1,0:T(8,128)(2,1)} %constant.62.clone.t2) | copy-start | bytes 1572868
  22.9 10.9 %copy-start.5 = (bf16[384,512]{1,0:T(8,128)(2,1)S(1)}, bf16[384,512]{1,0:T(8,128)(2,1)}, u32[]{:S(2)}) copy-start(bf16[384,512]{1,0:T(8,128)(2,1)} %constant.65.clone.yf) | copy-start | bytes 1179652
  22.9 10.9 %copy-start.6 = (bf16[256,512]{1,0:T(8,128)(2,1)S(1)}, bf16[256,512]{1,0:T(8,128)(2,1)}, u32[]{:S(2)}) copy-start(bf16[256,512]{1,0:T(8,128)(2,1)} %constant.63.clone.t3) | copy-start | bytes 786436
  22.9 10.9 %copy-start.11 = (bf16[256,48]{1,0:T(8,128)(2,1)S(1)}, bf16[256,48]{1,0:T(8,128)(2,1)}, u32[]{:S(2)}) copy-start(bf16[256,48]{1,0:T(8,128)(2,1)} %constant.64.clone.xf) | copy-start | bytes 73732
